TPU v7x, 256 devices: a whole 4x4x8 slice. The times are simulated.
256 devices in a mesh: rows: 32 (over z, x), cols: 8 (over y, core).
Axes of the slice: x: 4, y: 4, z: 8, core: 2. Of those that a mesh axis runs over, the one named last changes fastest.
Arguments:
- coupling: float32 [2, 16384, 16384], P(None, 'rows', 'cols'), may hold values from -2 to 40, as said below
- initial: float32 [2, 48, 16384], P(None, None, 'rows'), may hold values from -8 to 8
Outputs:
- basis: float32 [2, 48, 16384], P(None, None, ('rows', 'cols'))
- ritz: float32 [4, 2, 48, 48], replicated
Inputs may be any that keep to these rules, and one draw needn't show every extreme that they name: `coupling`: H is Hermitian (the first plane symmetric, the second antisymmetric) and positive definite.
All inputs are finite; a program needn't handle non-finite values.
Results may differ from a plain program's by a relative error of at most 0.0003.
Values sent between devices are 32-bit elements; how exact they have to be, the bound alone decides.
A program may use at most 64 MiB of HBM per device.

v0:
```python
import jax
import jax.numpy as jnp
from jax import lax
from jax.sharding import Mesh
from jax.sharding import PartitionSpec as P

N = 16384
ITERS = 4
ROWS = ("rows_0", "rows_1")
ROWS_COLS = ("rows_0", "rows_1", "cols")


HIGH = lax.Precision.HIGHEST


def gathered_by_axis(value, axes, dim):
    if not axes:
        return value
    nearer = lax.all_gather(value, axes[-1], axis=dim, tiled=True)
    return gathered_by_axis(nearer, axes[:-1], dim)


def copy_for_each(value, axis):
    copies = jnp.broadcast_to(value, (lax.axis_size(axis), *value.shape))
    return lax.all_to_all(copies, axis, split_axis=0, concat_axis=0, tiled=True)


def of_everyone(value, axis):
    everything = copy_for_each(value, axis)
    return jnp.sum(everything, axis=0)


def in_one(arrays, axis):
    vector, at, gathered = (jnp.concatenate([a.reshape(-1) for a in arrays]), 0, [])
    total = of_everyone(vector, axis)
    for a in arrays:
        gathered.append(total[at : at + a.size].reshape(a.shape))
        at += a.size
    return tuple(gathered)


def pair_products(left, right):
    real_part = jnp.dot(left[0], right[0].T, precision=HIGH) + jnp.dot(
        left[1], right[1].T, precision=HIGH
    )
    imag_part = jnp.dot(left[0], right[1].T, precision=HIGH) - jnp.dot(
        left[1], right[0].T, precision=HIGH
    )
    return jnp.stack([real_part, imag_part])


def orthonormal(gram_matrix, images):
    gram_re = gram_matrix[0]
    gram_im = gram_matrix[1]
    vectors = gram_re.shape[0]
    width = images.shape[2]
    upper_pair = jnp.stack([gram_re, -gram_im], axis=-1)
    lower_pair = jnp.stack([gram_im, gram_re], axis=-1)
    embedded = jnp.stack([upper_pair, lower_pair], axis=1).reshape(2 * vectors, 2 * vectors)
    factor = jnp.linalg.cholesky(embedded)
    woven = jnp.transpose(images, (1, 0, 2)).reshape(2 * vectors, width)
    solved = lax.linalg.triangular_solve(factor, woven, left_side=True, lower=True)
    return jnp.transpose(solved.reshape(vectors, 2, width), (1, 0, 2))


def tile_product(coupling, local_block):
    vectors = local_block.shape[1]
    stacked = local_block.reshape(2 * vectors, local_block.shape[2])
    contract = (((1,), (1,)), ((), ()))
    with_real = lax.dot_general(
        stacked, coupling[0], contract, precision=HIGH, preferred_element_type=jnp.float32
    )
    with_imag = lax.dot_general(
        stacked, coupling[1], contract, precision=HIGH, preferred_element_type=jnp.float32
    )
    return jnp.stack(
        [with_real[:vectors] - with_imag[vectors:], with_real[vectors:] + with_imag[:vectors]]
    )


def body(coupling, initial):
    row_width = initial.shape[2]
    per_column = lax.axis_size(ROWS) // lax.axis_size("cols")
    column = lax.axis_index("cols")
    block_span = row_width * per_column
    piece_width = row_width // lax.axis_size("cols")
    order_value = float(N)
    ritz_list = []
    current = initial
    for iteration in range(ITERS):
        gathered = gathered_by_axis(current, ROWS, 2)
        local_block = lax.dynamic_slice_in_dim(gathered, column * block_span, block_span, 2)
        partial_value = tile_product(coupling, local_block)
        images = of_everyone(partial_value, "cols")
        gram_matrix, projection = in_one(
            (pair_products(images, images), pair_products(current, images)), ROWS
        )
        ritz_list.append(projection / order_value)
        current = orthonormal(gram_matrix / order_value, images)
    final_piece = lax.dynamic_slice_in_dim(current, column * piece_width, piece_width, 2)
    return (final_piece, jnp.stack(ritz_list))


def solution(mesh):
    torus = Mesh(mesh.devices.reshape(8, 4, mesh.shape["cols"]), ("rows_0", "rows_1", "cols"))
    in_specs = (P(None, ROWS, "cols"), P(None, None, ROWS))
    out_specs = (P(None, None, ROWS_COLS), P())
    return jax.shard_map(body, mesh=torus, in_specs=in_specs, out_specs=out_specs, check_vma=False)
```

profile of v0, /device:TPU:1, one launch (start us, length us, event | category | flops | bytes accessed | tf_op | source)
XLA Modules:
  0.0 769.0 jit_solution(13213316916078772046)
XLA Ops:
  7.2 14.1 %all_gather.24 = f32[2,48,2048]{2,1,0:T(8,128)} all-gather(f32[2,48,512]{2,1,0:T(8,128)} %param.6), channel_id=1, replica_groups=mesh['rows_0'=8,'rows_1'=4,'cols'=8] {'rows_1'}, dimensions={2}, use_global_device_ids=true | all-gather | bytes 983040 | tf_op jit(solution)/shard_map/all_gather | solution.py:19
  21.4 78.8 %all-gather.5.cloned.1.call-done = f32[2,48,16384]{2,1,0:T(8,128)} async-done(((f32[2,48,2048]{2,1,0:T(8,128)}), f32[2,48,16384]{2,1,0:T(8,128)}) %all-gather.5.cloned.1.call-update) | async-done | bytes 6291472 | tf_op jit(solution)/shard_map/all_gather | solution.py:19
  114.3 25.6 %all_to_all.44 = f32[8,2,48,512]{3,2,1,0:T(8,128)S(1)} all-to-all(f32[8,2,48,512]{3,2,1,0:T(8,128)S(1)} %broadcast_in_dim.25), channel_id=1, replica_groups=mesh['rows_0'=8,'rows_1'=4,'cols'=8] {'cols'}, dimensions={0} | all-to-all | bytes 3145728 | tf_op jit(solution)/shard_map/all_to_all | solution.py:25
  151.2 27.8 %all-to-all-done.1 = f32[32,1,9216]{2,1,0:T(1,128)S(1)} async-done(((f32[32,1,9216]{2,1,0:T(1,128)}), f32[32,1,9216]{2,1,0:T(1,128)S(1)}, u32[]{:S(2)}, u32[]{:S(2)}) %all-to-all-start.1) | async-done | bytes 1179680 | tf_op jit(solution)/shard_map/all_to_all | solution.py:25
  181.9 8.8 %cholesky.74 = f32[96,96]{1,0:T(8,128)S(1)} custom-call(f32[96,96]{1,0:T(8,128)S(1)} %fusion.87), custom_call_target="Cholesky" | custom-call | tf_op jit(solution)/shard_map/jit(cholesky)/cholesky | solution.py:60
  192.0 7.4 custom-call.8
  199.9 13.2 %all_gather.26 = f32[2,48,2048]{2,1,0:T(8,128)} all-gather(f32[2,48,512]{2,1,0:T(8,128)S(1)} %bitcast.269), channel_id=1, replica_groups=mesh['rows_0'=8,'rows_1'=4,'cols'=8] {'rows_1'}, dimensions={2}, use_global_device_ids=true | all-gather | bytes 983040 | tf_op jit(solution)/shard_map/all_gather | solution.py:19
  213.1 73.9 %all-gather.7.cloned.1.call-done = f32[2,48,16384]{2,1,0:T(8,128)} async-done(((f32[2,48,2048]{2,1,0:T(8,128)}), f32[2,48,16384]{2,1,0:T(8,128)}) %all-gather.7.cloned.1.call-update) | async-done | bytes 6291472 | tf_op jit(solution)/shard_map/all_gather | solution.py:19
  301.1 25.6 %all_to_all.45 = f32[8,2,48,512]{3,2,1,0:T(8,128)S(1)} all-to-all(f32[8,2,48,512]{3,2,1,0:T(8,128)S(1)} %broadcast_in_dim.27), channel_id=1, replica_groups=mesh['rows_0'=8,'rows_1'=4,'cols'=8] {'cols'}, dimensions={0} | all-to-all | bytes 3145728 | tf_op jit(solution)/shard_map/all_to_all | solution.py:25
  338.2 27.6 %all-to-all-done.3 = f32[32,1,9216]{2,1,0:T(1,128)S(1)} async-done(((f32[32,1,9216]{2,1,0:T(1,128)}), f32[32,1,9216]{2,1,0:T(1,128)S(1)}, u32[]{:S(2)}, u32[]{:S(2)}) %all-to-all-start.3) | async-done | bytes 1179680 | tf_op jit(solution)/shard_map/all_to_all | solution.py:25
  368.7 8.8 %cholesky.85 = f32[96,96]{1,0:T(8,128)S(1)} custom-call(f32[96,96]{1,0:T(8,128)S(1)} %fusion.84), custom_call_target="Cholesky" | custom-call | tf_op jit(solution)/shard_map/jit(cholesky)/cholesky | solution.py:60
  378.8 7.4 custom-call.9
  386.7 13.1 %all_gather.28 = f32[2,48,2048]{2,1,0:T(8,128)} all-gather(f32[2,48,512]{2,1,0:T(8,128)S(1)} %bitcast.274), channel_id=1, replica_groups=mesh['rows_0'=8,'rows_1'=4,'cols'=8] {'rows_1'}, dimensions={2}, use_global_device_ids=true | all-gather | bytes 983040 | tf_op jit(solution)/shard_map/all_gather | solution.py:19
  399.8 73.9 %all-gather.9.cloned.1.call-done = f32[2,48,16384]{2,1,0:T(8,128)} async-done(((f32[2,48,2048]{2,1,0:T(8,128)}), f32[2,48,16384]{2,1,0:T(8,128)}) %all-gather.9.cloned.1.call-update) | async-done | bytes 6291472 | tf_op jit(solution)/shard_map/all_gather | solution.py:19
  487.8 25.6 %all_to_all.46 = f32[8,2,48,512]{3,2,1,0:T(8,128)S(1)} all-to-all(f32[8,2,48,512]{3,2,1,0:T(8,128)S(1)} %broadcast_in_dim.29), channel_id=1, replica_groups=mesh['rows_0'=8,'rows_1'=4,'cols'=8] {'cols'}, dimensions={0} | all-to-all | bytes 3145728 | tf_op jit(solution)/shard_map/all_to_all | solution.py:25
  524.7 27.8 %all-to-all-done.5 = f32[32,1,9216]{2,1,0:T(1,128)S(1)} async-done(((f32[32,1,9216]{2,1,0:T(1,128)}), f32[32,1,9216]{2,1,0:T(1,128)S(1)}, u32[]{:S(2)}, u32[]{:S(2)}) %all-to-all-start.5) | async-done | bytes 1179680 | tf_op jit(solution)/shard_map/all_to_all | solution.py:25
  555.3 8.8 %cholesky.96 = f32[96,96]{1,0:T(8,128)S(1)} custom-call(f32[96,96]{1,0:T(8,128)S(1)} %fusion.81), custom_call_target="Cholesky" | custom-call | tf_op jit(solution)/shard_map/jit(cholesky)/cholesky | solution.py:60
  565.5 7.4 custom-call.10
  573.4 13.2 %all_gather.30 = f32[2,48,2048]{2,1,0:T(8,128)} all-gather(f32[2,48,512]{2,1,0:T(8,128)S(1)} %bitcast.264), channel_id=1, replica_groups=mesh['rows_0'=8,'rows_1'=4,'cols'=8] {'rows_1'}, dimensions={2}, use_global_device_ids=true | all-gather | bytes 983040 | tf_op jit(solution)/shard_map/all_gather | solution.py:19
  586.6 73.9 %all-gather.11.cloned.1.call-done = f32[2,48,16384]{2,1,0:T(8,128)} async-done(((f32[2,48,2048]{2,1,0:T(8,128)}), f32[2,48,16384]{2,1,0:T(8,128)}) %all-gather.11.cloned.1.call-update) | async-done | bytes 6291472 | tf_op jit(solution)/shard_map/all_gather | solution.py:19
  674.6 25.6 %all_to_all.47 = f32[8,2,48,512]{3,2,1,0:T(8,128)S(1)} all-to-all(f32[8,2,48,512]{3,2,1,0:T(8,128)S(1)} %broadcast_in_dim.31), channel_id=1, replica_groups=mesh['rows_0'=8,'rows_1'=4,'cols'=8] {'cols'}, dimensions={0} | all-to-all | bytes 3145728 | tf_op jit(solution)/shard_map/all_to_all | solution.py:25
  711.8 27.8 %all-to-all-done.7 = f32[32,1,9216]{2,1,0:T(1,128)S(1)} async-done(((f32[32,1,9216]{2,1,0:T(1,128)}), f32[32,1,9216]{2,1,0:T(1,128)S(1)}, u32[]{:S(2)}, u32[]{:S(2)}) %all-to-all-start.7) | async-done | bytes 1179680 | tf_op jit(solution)/shard_map/all_to_all | solution.py:25
  742.5 8.8 %cholesky.107 = f32[96,96]{1,0:T(8,128)S(1)} custom-call(f32[96,96]{1,0:T(8,128)S(1)} %fusion.78), custom_call_target="Cholesky" | custom-call | tf_op jit(solution)/shard_map/jit(cholesky)/cholesky | solution.py:60
  752.6 7.4 custom-call.11
  (185 shorter events, 121.7 us)
Async XLA Ops:
  7.2 93.0 %all-gather.5.cloned.1.call-start = ((), (), s32[]{:S(2)}) async-start(), calls=%async_computation.8 | async-start | bytes 7077888 | tf_op jit(solution)/shard_map/all_gather | solution.py:19
  114.0 26.4 %copy-start = (f32[2,48,512]{2,1,0:T(8,128)S(1)}, f32[2,48,512]{2,1,0:T(8,128)}, u32[]{:S(2)}) copy-start(f32[2,48,512]{2,1,0:T(8,128)} %param.6) | copy-start | bytes 589828
  143.8 35.2 %all-to-all-start.1 = ((f32[32,1,9216]{2,1,0:T(1,128)}), f32[32,1,9216]{2,1,0:T(1,128)S(1)}, u32[]{:S(2)}, u32[]{:S(2)}) async-start(f32[32,1,9216]{2,1,0:T(1,128)} %broadcast_in_dim.26), calls=%async_computation.1 | async-start | bytes 2359296 | tf_op jit(solution)/shard_map/all_to_all | solution.py:25
  150.7 136.4 %all-gather.7.cloned.1.call-start = ((), (), s32[]{:S(2)}) async-start(), calls=%async_computation.9 | async-start | bytes 7077888 | tf_op jit(solution)/shard_map/all_gather | solution.py:19
  330.6 35.2 %all-to-all-start.3 = ((f32[32,1,9216]{2,1,0:T(1,128)}), f32[32,1,9216]{2,1,0:T(1,128)S(1)}, u32[]{:S(2)}, u32[]{:S(2)}) async-start(f32[32,1,9216]{2,1,0:T(1,128)} %broadcast_in_dim.28), calls=%async_computation.3 | async-start | bytes 2359296 | tf_op jit(solution)/shard_map/all_to_all | solution.py:25
  337.4 136.3 %all-gather.9.cloned.1.call-start = ((), (), s32[]{:S(2)}) async-start(), calls=%async_computation.10 | async-start | bytes 7077888 | tf_op jit(solution)/shard_map/all_gather | solution.py:19
  517.3 35.2 %all-to-all-start.5 = ((f32[32,1,9216]{2,1,0:T(1,128)}), f32[32,1,9216]{2,1,0:T(1,128)S(1)}, u32[]{:S(2)}, u32[]{:S(2)}) async-start(f32[32,1,9216]{2,1,0:T(1,128)} %broadcast_in_dim.30), calls=%async_computation.5 | async-start | bytes 2359296 | tf_op jit(solution)/shard_map/all_to_all | solution.py:25
  524.1 136.4 %all-gather.11.cloned.1.call-start = ((), (), s32[]{:S(2)}) async-start(), calls=%async_computation.11 | async-start | bytes 7077888 | tf_op jit(solution)/shard_map/all_gather | solution.py:19
  704.1 35.5 %all-to-all-start.7 = ((f32[32,1,9216]{2,1,0:T(1,128)}), f32[32,1,9216]{2,1,0:T(1,128)S(1)}, u32[]{:S(2)}, u32[]{:S(2)}) async-start(f32[32,1,9216]{2,1,0:T(1,128)} %broadcast_in_dim.32), calls=%async_computation.7 | async-start | bytes 2359296 | tf_op jit(solution)/shard_map/all_to_all | solution.py:25
Sparse Core Ops, SparseCore 0:
  21.5 78.6 all-gather.4
  213.2 73.7 all-gather.6
  399.9 73.7 all-gather.8
  586.7 73.7 all-gather.10
where the time goes:
time: 779 us; the launch traced here: 769 us
  waiting for transfers between devices  412 us (53%)
  blocking collectives  156 us (20%)
  other arithmetic  74.3 us (10%)
  matrix products  59.4 us (8%)
  starting transfers between devices  28.7 us (4%)
  local copies, waits for them, and re-layouts  23.7 us (3%)
  between operations  15.3 us (2%)
    all_gather x4, waiting for transfers between devices, gathered_by_axis(): nearer = lax.all_gather(value, axes[-1], axis=dim, tiled=True)  300 us
    all_to_all x4, waiting for transfers between devices, copy_for_each(): return lax.all_to_all(copies, axis, split_axis=0, concat_axis=0, tiled=True)  111 us
    all_to_all x4, blocking collectives, copy_for_each(): return lax.all_to_all(copies, axis, split_axis=0, concat_axis=0, tiled=True)  102 us
    all_gather x4, blocking collectives, gathered_by_axis(): nearer = lax.all_gather(value, axes[-1], axis=dim, tiled=True)  53.7 us
    another operation x12, other arithmetic, orthonormal(): factor = jnp.linalg.cholesky(embedded)  37.8 us
    another operation x8, other arithmetic, orthonormal(): lax.linalg.triangular_solve(factor, woven, left_side=True, lower=True)  32 us
    all_to_all x4, starting transfers between devices, copy_for_each(): return lax.all_to_all(copies, axis, split_axis=0, concat_axis=0, tiled=True)  27.7 us
    dot_general x4, matrix products, tile_product(): lax.dot_general(stacked, coupling[1], contract, precision=HIGH, preferred...  25.3 us
  transfers between devices with their start and end apart: 8, of which 8 were waited for; matrix products, arithmetic and copies ran while one was open for 0% of the time, Pallas kernels for 0%

commit v1 on v0

v1 whole, which is shorter than its diff:
```python
import jax
import jax.numpy as jnp
from jax import lax
from jax.experimental import pallas as pl
from jax.experimental.pallas import tpu as pltpu
from jax.sharding import PartitionSpec as P

N = 16384
K = 48
ITERS = 4
X, Z, C = 4, 8, 8
CH = 256
RB = 2 * K // X
F32, BF16 = jnp.float32, jnp.bfloat16
MESH = pl.DeviceIdType.MESH
HIGH = lax.Precision.HIGHEST
NT = (((1,), (1,)), ((), ()))


def dot(a, b, precision=None):
    return jnp.dot(a, b, precision=precision, preferred_element_type=F32)


def dot_nt(a, b, precision=None):
    return lax.dot_general(a, b, NT, precision=precision, preferred_element_type=F32)


def split(value):
    high = value.astype(BF16)
    return high, (value - high.astype(F32)).astype(BF16)


def lanes(shape):
    return lax.broadcasted_iota(jnp.int32, shape, 1)


def turned(packed):
    rolled = pltpu.roll(packed, 64, 1)
    return jnp.where(lanes(packed.shape) < 64, rolled, -rolled)


def stacked_rows(first, second):
    gap = jnp.zeros((64 - K, first.shape[1]), first.dtype)
    return jnp.concatenate([first, gap, second, gap], axis=0)


def gram_packed(left, right):
    return dot_nt(left, stacked_rows(right, turned(right)), HIGH)


def gram_planes(re, im):
    return dot_nt(re, stacked_rows(re, im), HIGH) + dot_nt(im, stacked_rows(im, -re), HIGH)


def planes_of(packed):
    low = lanes(packed.shape) < 64
    return jnp.where(low, packed, 0.0), jnp.where(low, pltpu.roll(packed, 64, 1), 0.0)


def apply_packed(matrix, packed):
    re, im = planes_of(matrix)
    return dot(re[:, :K], packed, HIGH) - dot(im[:, :K], turned(packed), HIGH)


def conj_apply_packed(matrix, packed):
    re, im = planes_of(matrix)
    return dot(re[:, :K], packed, HIGH) + dot(im[:, :K], turned(packed), HIGH)


def embedded(matrix):
    re, im = planes_of(matrix)
    upper = re - pltpu.roll(im, K, 1)
    lower = im + pltpu.roll(re, K, 1)
    return jnp.concatenate([upper, lower], axis=0)[:, : 2 * K]


def inverse_factor(gram):
    lane = lanes((K, 128))
    row = lax.broadcasted_iota(jnp.int32, (K, 128), 0)
    low = lane < 64
    re = jnp.where(low, gram, jnp.where(lane - 64 == row, 1.0, 0.0))
    im = jnp.where(low, pltpu.roll(gram, 64, 1), 0.0)
    done_re, done_im = [], []
    for base in range(0, K, 8):
        below = lax.broadcasted_iota(jnp.int32, (K - base, 1), 0)
        for s in range(8):
            j = base + s
            row_re, row_im = re[s : s + 1], im[s : s + 1]
            inv = 1.0 / re[s : s + 1, j : j + 1]
            m_re = jnp.where(below > s, re[:, j : j + 1] * inv, 0.0)
            m_im = jnp.where(below > s, im[:, j : j + 1] * inv, 0.0)
            re, im = (
                re - (m_re * row_re - m_im * row_im),
                im - (m_re * row_im + m_im * row_re),
            )
        done_re.append(re[:8])
        done_im.append(im[:8])
        re, im = re[8:], im[8:]
    re = jnp.concatenate(done_re, axis=0)
    im = jnp.concatenate(done_im, axis=0)
    pivot = jnp.sum(jnp.where(lane == row, re, 0.0), axis=1, keepdims=True)
    scale = 1.0 / jnp.sqrt(pivot)
    return jnp.where(low, pltpu.roll(re, 64, 1), im) * scale


def pack_pair(re, im):
    low = lanes(re.shape) < 64
    even = jnp.where(low, re, pltpu.roll(im, 64, 1))
    odd = jnp.where(low, pltpu.roll(re, 64, 1), im)
    return even, odd


def unpack_pair(even, odd):
    low = lanes(even.shape) < 64
    re = jnp.where(low, even, pltpu.roll(odd, 64, 1))
    im = jnp.where(low, pltpu.roll(even, 64, 1), odd)
    return re, im


def far_first(k):
    return 4 + (k // 2) * (1 - k % 2) - ((k + 1) // 2) * (k % 2)


def near_first(k):
    return (8 + far_first(7 - k)) % 8


def kernel(coupling, initial, basis, ritz, *scratch):
    (
        stage, hhi, hlo, lhs, part, rsx, red, rsz, gath, ybuf, ysplit, acc, acc2,
        pk, rsy, gy, scat, ypc, gsrc, gyc, gxs, gx, gzs, gz,
        fsrc, fy, fxs, fx, fzs, fz, fall,
        hsem, rsx_s, rsx_r, rsz_s, rsz_r, agz_s, agz_r, agx_s, agx_r,
        rsy_s, rsy_r, agy_s, agy_r, sc_s, sc_r, gyc_s, gyc_r, gx_s, gx_r, gz_s, gz_r,
        fy_s, fy_r, fx_s, fx_r, fz_s, fz_r, fa_s, fa_r,
    ) = scratch
    r, c = lax.axis_index("rows"), lax.axis_index("cols")
    z, x = r // X, r % X

    def at_x(j):
        return (z * X + (x + j) % X, c)

    def at_z(o):
        return (((z + o) % Z) * X + x, c)

    def at_c(k):
        return (r, (c + k) % C)

    def remote(src, dst, send, recv, dev):
        return pltpu.make_async_remote_copy(
            src_ref=src, dst_ref=dst, send_sem=send, recv_sem=recv,
            device_id=dev, device_id_type=MESH,
        )

    def loop(n, f):
        def step(i, carry):
            f(i)
            return carry

        lax.fori_loop(0, n, step, 0)

    def rows_of(j):
        return pl.ds(pl.multiple_of(((x + j) % X) * RB, 8), RB)

    def load(k):
        zc = (z + far_first(k)) % Z
        columns = pl.ds(pl.multiple_of(zc * CH, CH), CH)
        return pltpu.make_async_copy(coupling.at[:, :, columns], stage.at[zc], hsem.at[zc])

    loop(Z, lambda k: load(k).start())

    barrier = pltpu.get_barrier_semaphore()
    partners = [at_x(j) for j in range(1, X)] + [at_z(o) for o in range(1, Z)]
    partners += [at_c(k) for k in range(1, C)]
    for dev in partners:
        pl.semaphore_signal(barrier, inc=1, device_id=dev, device_id_type=MESH)

    def set_left(re, im):
        top = jnp.concatenate([re, im], axis=1)
        bottom = jnp.concatenate([im, -re], axis=1)
        high, low = split(jnp.concatenate([top, bottom], axis=0))
        lhs[...] = jnp.concatenate([high, low], axis=0)

    v_re, v_im = initial[0], initial[1]
    set_left(v_re, v_im)
    for t in range(4):
        even, odd = pack_pair(v_re[:, 128 * t : 128 * t + 128], v_im[:, 128 * t : 128 * t + 128])
        pk[2 * t], pk[2 * t + 1] = even, odd
    v_piece = pk[c]
    pl.semaphore_wait(barrier, len(partners))


    def x_part(j, zc):
        return remote(
            part.at[zc, rows_of(j)], rsx.at[j - 1, zc], rsx_s.at[j - 1, zc], rsx_r.at[j - 1, zc], at_x(j)
        )

    def z_part(o, zc):
        return remote(red.at[zc], rsz.at[o], rsz_s.at[o], rsz_r.at[o], at_z(o))

    def column_product(first):
        def chunk(k):
            zc = (z + far_first(k)) % Z
            if first:
                load(k).wait()
                for t in range(0, 1024, 128):
                    high, low = split(stage[zc, t // 512, t % 512 : t % 512 + 128])
                    hhi[zc, t : t + 128] = high
                    hlo[zc, t : t + 128] = low
            both = dot(lhs[...], hhi[zc])
            rest = dot(lhs[: 2 * K], hlo[zc])
            part[zc] = both[: 2 * K] + both[2 * K :] + rest
            for j in range(1, X):
                x_part(j, zc).start()

        loop(Z, chunk)

    def column_sum():
        def chunk(k):
            o = far_first(k)
            zc = (z + o) % Z
            total = part[zc, rows_of(0)]
            for j in range(1, X):
                x_part(j, zc).wait_recv()
                total = total + rsx[j - 1, zc]
            red[zc] = total

            @pl.when(k < Z - 1)
            def _():
                z_part(o, zc).start()

        loop(Z, chunk)
        total = red[z]
        for o in range(1, Z):
            z_part(o, z).wait_recv()
            total = total + rsz[o]
        return total

    def column_sum_sent():
        def chunk(k):
            o = far_first(k)
            zc = (z + o) % Z
            for j in range(1, X):
                x_part(j, zc).wait_send()

            @pl.when(k < Z - 1)
            def _():
                z_part(o, zc).wait_send()

        loop(Z, chunk)


    def z_whole(o, zc):
        block = gath.at[zc, rows_of(0)]
        return remote(block, block, agz_s.at[o], agz_r.at[o], at_z(o))

    def x_whole(j, zc, shift):
        block = gath.at[zc, rows_of(shift)]
        return remote(block, block, agx_s.at[j - 1, zc], agx_r.at[j - 1, zc], at_x(j))

    def column_gather(total):
        gath[z, rows_of(0)] = total
        loop(Z - 1, lambda k: z_whole(far_first(k), z).start())

        def forward(k):
            o = near_first(k)
            zc = (z + Z - o) % Z

            @pl.when(k > 0)
            def _():
                z_whole(o, zc).wait_recv()

            for j in range(1, X):
                x_whole(j, zc, 0).start()

        loop(Z, forward)

    def column_gather_sent():
        loop(Z - 1, lambda k: z_whole(far_first(k), z).wait_send())

        def chunk(zc):
            for j in range(1, X):
                x_whole(j, zc, 0).wait_send()

        loop(Z, chunk)

    def c_gram(h, k):
        return remote(gsrc, gyc.at[h, k], gyc_s.at[h, k], gyc_r.at[h, k], at_c(k))

    def c_scatter(h, k):
        return remote(scat.at[h, (c + k) % C], ypc.at[h], sc_s.at[h, k], sc_r.at[h], at_c(k))

    def row_product(h, factor):
        def receive(k, gram):
            zc = (z + Z - near_first(k)) % Z
            for j in range(1, X):
                x_whole(j, zc, -j).wait_recv()
            block = gath[zc]
            if factor is not None:
                block = dot(factor, block, HIGH)
            ybuf[zc] = block
            high, low = split(block)
            ysplit[zc] = jnp.concatenate([high, low], axis=0)
            return gram + gram_planes(block[:K], block[K:])

        gsrc[...] = lax.fori_loop(0, Z, receive, jnp.zeros((K, 128), F32))
        for k in range(1, C):
            c_gram(h, k).start()

        @pl.when(c == z)
        def _():
            for t in range(4):
                chunk = ybuf.at[2 * x + t // 2]
                part_lanes = slice((t % 2) * 128, (t % 2) * 128 + 128)
                even, odd = pack_pair(chunk[:K, part_lanes], chunk[K:, part_lanes])
                scat[h, 2 * t], scat[h, 2 * t + 1] = even, odd
            for k in range(1, C):
                c_scatter(h, k).start()
            ypc[h] = scat[h, c]

        acc[...] = jnp.zeros_like(acc)
        acc2[...] = jnp.zeros_like(acc2)

        def chunk(k):
            acc[...] += dot_nt(ysplit[k], hhi[k])
            acc2[...] += dot_nt(ysplit[k, : 2 * K], hlo[k])

        loop(Z, chunk)
        total = acc[: 2 * K] + acc[2 * K :] + acc2[...]
        re = total[:K, :512] - total[K:, 512:]
        im = total[K:, :512] + total[:K, 512:]
        for t in range(4):
            even, odd = pack_pair(re[:, 128 * t : 128 * t + 128], im[:, 128 * t : 128 * t + 128])
            pk[2 * t], pk[2 * t + 1] = even, odd

    def c_part(k):
        return remote(pk.at[(c + k) % C], rsy.at[k], rsy_s.at[k], rsy_r.at[k], at_c(k))

    def row_sum_start():
        for k in range(1, C):
            c_part(k).start()

    def row_sum():
        total = pk[c]
        for k in range(1, C):
            c_part(k).wait_recv()
            total = total + rsy[k]
        return total

    def c_factor(h):
        total = gsrc[...]
        for k in range(1, C):
            c_gram(h, k).wait_recv()
            total = total + gyc[h, k]
        return inverse_factor(total * (1.0 / N))

    def scattered(h):
        @pl.when(c != z)
        def _():
            c_scatter(h, 1).wait_recv()

        return ypc[h]

    def row_product_sent(h):
        for k in range(1, C):
            c_part(k).wait_send()
            c_gram(h, k).wait_send()

        @pl.when(c == z)
        def _():
            for k in range(1, C):
                c_scatter(h, k).wait_send()

    column_product(True)
    column_gather(column_sum())
    row_product(0, None)
    row_sum_start()
    z2_piece = row_sum()
    gy[c] = z2_piece

    def c_whole(k, src):
        return remote(gy.at[src], gy.at[src], agy_s.at[k], agy_r.at[k], at_c(k))

    for k in range(1, C):
        c_whole(k, c).start()
    inv1 = c_factor(0)
    y1_piece = scattered(0)
    y2_piece = apply_packed(inv1, z2_piece)
    fsrc[K : 2 * K] = gram_packed(v_piece, y1_piece)
    fsrc[2 * K : 3 * K] = conj_apply_packed(inv1, gram_packed(y1_piece, y2_piece))
    for k in range(1, C):
        c_whole(k, (c + C - k) % C).wait_recv()
    re, im = [], []
    for t in range(4):
        pair_re, pair_im = unpack_pair(gy[2 * t], gy[2 * t + 1])
        re.append(pair_re)
        im.append(pair_im)
    block = jnp.concatenate([jnp.concatenate(re, axis=1), jnp.concatenate(im, axis=1)], axis=0)
    block = dot(embedded(inv1), block, HIGH)
    y2_re, y2_im = block[:K], block[K:]
    set_left(y2_re, y2_im)
    gxs[...] = gram_planes(y2_re, y2_im)

    def x_gram(j):
        return remote(gxs, gx.at[j], gx_s.at[j], gx_r.at[j], at_x(j))

    def z_gram(o):
        return remote(gzs, gz.at[o], gz_s.at[o], gz_r.at[o], at_z(o))

    for j in range(1, X):
        x_gram(j).start()
    column_sum_sent()
    column_gather_sent()
    row_product_sent(0)
    column_product(False)
    total = gxs[...]
    for j in range(1, X):
        x_gram(j).wait_recv()
        total = total + gx[j]
    gzs[...] = total
    for o in range(1, Z):
        z_gram(o).start()
    column_gather(column_sum())
    total = gzs[...]
    for o in range(1, Z):
        z_gram(o).wait_recv()
        total = total + gz[o]
    inv2 = inverse_factor(total * (1.0 / N))
    row_product(1, embedded(inv2))
    row_sum_start()
    inv3 = c_factor(1)
    y3_piece = scattered(1)
    fsrc[3 * K : 4 * K] = conj_apply_packed(inv2, gram_packed(y2_piece, y3_piece))
    y4_piece = apply_packed(inv3, row_sum())
    fsrc[:K] = gram_packed(y4_piece, y4_piece)
    fsrc[4 * K : 5 * K] = conj_apply_packed(inv3, gram_packed(y3_piece, y4_piece))
    fsrc[5 * K :] = jnp.zeros((256 - 5 * K, 128), F32)


    def slab(k):
        return pl.ds(pl.multiple_of(((c + k) % C) * 32, 32), 32)

    def f_c(k):
        return remote(fsrc.at[slab(k)], fy.at[k], fy_s.at[k], fy_r.at[k], at_c(k))

    def f_x(j):
        return remote(fxs, fx.at[j], fx_s.at[j], fx_r.at[j], at_x(j))

    def f_z(o):
        return remote(fzs, fz.at[o], fz_s.at[o], fz_r.at[o], at_z(o))

    def f_all(k, shift):
        return remote(fall.at[slab(shift)], fall.at[slab(shift)], fa_s.at[k], fa_r.at[k], at_c(k))

    for k in range(1, C):
        f_c(k).start()
    total = fsrc[slab(0)]
    for k in range(1, C):
        f_c(k).wait_recv()
        total = total + fy[k]
    fxs[...] = total
    for j in range(1, X):
        f_x(j).start()
    for j in range(1, X):
        f_x(j).wait_recv()
        total = total + fx[j]
    fzs[...] = total
    for o in range(1, Z):
        f_z(o).start()
    for o in range(1, Z):
        f_z(o).wait_recv()
        total = total + fz[o]
    fall[slab(0)] = total * (1.0 / N)
    for k in range(1, C):
        f_all(k, 0).start()
    for k in range(1, C):
        f_all(k, C - k).wait_recv()
    value = apply_packed(inverse_factor(fall[:K]), y4_piece)
    basis[0] = value[:, :64]
    basis[1] = pltpu.roll(value, 64, 1)[:, :64]
    for t in range(ITERS):
        value = fall[K * (t + 1) : K * (t + 2)]
        ritz[t, 0] = value[:, :K]
        ritz[t, 1] = pltpu.roll(value, 64, 1)[:, :K]

    column_sum_sent()
    column_gather_sent()
    row_product_sent(1)
    for k in range(1, C):
        c_whole(k, c).wait_send()
        f_c(k).wait_send()
        f_all(k, 0).wait_send()
    for j in range(1, X):
        x_gram(j).wait_send()
        f_x(j).wait_send()
    for o in range(1, Z):
        z_gram(o).wait_send()
        f_z(o).wait_send()


def solution(mesh):
    dma = pltpu.SemaphoreType.DMA
    packed = (K, 128)
    scratch = [
        pltpu.VMEM((Z, 2, 512, CH), F32),
        pltpu.VMEM((Z, 1024, CH), BF16),
        pltpu.VMEM((Z, 1024, CH), BF16),
        pltpu.VMEM((4 * K, 1024), BF16),
        pltpu.VMEM((Z, 2 * K, CH), F32),
        pltpu.VMEM((X - 1, Z, RB, CH), F32),
        pltpu.VMEM((Z, RB, CH), F32),
        pltpu.VMEM((Z, RB, CH), F32),
        pltpu.VMEM((Z, 2 * K, CH), F32),
        pltpu.VMEM((Z, 2 * K, CH), F32),
        pltpu.VMEM((Z, 4 * K, CH), BF16),
        pltpu.VMEM((4 * K, 1024), F32),
        pltpu.VMEM((2 * K, 1024), F32),
        pltpu.VMEM((C, *packed), F32),
        pltpu.VMEM((C, *packed), F32),
        pltpu.VMEM((C, *packed), F32),
        pltpu.VMEM((2, C, *packed), F32),
        pltpu.VMEM((2, *packed), F32),
        pltpu.VMEM(packed, F32),
        pltpu.VMEM((2, C, *packed), F32),
        pltpu.VMEM(packed, F32),
        pltpu.VMEM((X, *packed), F32),
        pltpu.VMEM(packed, F32),
        pltpu.VMEM((Z, *packed), F32),
        pltpu.VMEM((256, 128), F32),
        pltpu.VMEM((C, 32, 128), F32),
        pltpu.VMEM((32, 128), F32),
        pltpu.VMEM((X, 32, 128), F32),
        pltpu.VMEM((32, 128), F32),
        pltpu.VMEM((Z, 32, 128), F32),
        pltpu.VMEM((256, 128), F32),
        dma((Z,)),
        dma((X - 1, Z)), dma((X - 1, Z)), dma((Z,)), dma((Z,)),
        dma((Z,)), dma((Z,)), dma((X - 1, Z)), dma((X - 1, Z)),
        dma((C,)), dma((C,)), dma((C,)), dma((C,)),
        dma((2, C)), dma((2,)), dma((2, C)), dma((2, C)),
        dma((X,)), dma((X,)), dma((Z,)), dma((Z,)),
        dma((C,)), dma((C,)), dma((X,)), dma((X,)), dma((Z,)), dma((Z,)), dma((C,)), dma((C,)),
    ]
    vmem = pl.BlockSpec(memory_space=pltpu.VMEM)

    def body(coupling, initial):
        return pl.pallas_call(
            kernel,
            name="subspace",
            out_shape=(
                jax.ShapeDtypeStruct((2, K, 64), F32),
                jax.ShapeDtypeStruct((ITERS, 2, K, K), F32),
            ),
            in_specs=[pl.BlockSpec(memory_space=pl.ANY), vmem],
            out_specs=(vmem, vmem),
            scratch_shapes=scratch,
            compiler_params=pltpu.CompilerParams(
                collective_id=0, has_side_effects=True, vmem_limit_bytes=56 * 1024 * 1024
            ),
        )(coupling, initial)

    return jax.shard_map(
        body,
        mesh=mesh,
        in_specs=(P(None, "rows", "cols"), P(None, None, "rows")),
        out_specs=(P(None, None, ("rows", "cols")), P()),
        check_vma=False,
    )
```

time: 779 us -> 122 us (0.16); the launches traced: 769 us -> 122 us
  waiting for transfers between devices: 412 us -> 0 us
  blocking collectives: 156 us -> 0 us
  Pallas kernels: 0 us -> 118 us
  other arithmetic: 74.3 us -> 0 us
  matrix products: 59.4 us -> 0 us
  starting transfers between devices: 28.7 us -> 0 us
  local copies, waits for them, and re-layouts: 23.7 us -> 3.04 us
  between operations: 15.3 us -> 0.64 us
    all_gather x4 -> x0, waiting for transfers between devices: 300 us -> none  [gathered_by_axis(): nearer = lax.all_gather(value, axes[-1], axis=dim, tiled=True)]
    pallas_call x0 -> x1, Pallas kernels: none -> 118 us  [body(): pl.pallas_call(kernel, name='subspace', out_shape=(jax.ShapeDtypeStruct((...]
    all_to_all x4 -> x0, waiting for transfers between devices: 111 us -> none  [copy_for_each(): return lax.all_to_all(copies, axis, split_axis=0, concat_axis=0, tiled=True)]
    all_to_all x4 -> x0, blocking collectives: 102 us -> none  [copy_for_each(): return lax.all_to_all(copies, axis, split_axis=0, concat_axis=0, tiled=True)]
    another operation x45 -> x0, other arithmetic: 70.9 us -> none  [the longest x12 37.8 us: orthonormal(): factor = jnp.linalg.cholesky(embedded)]
    dot_general x40 -> x0, matrix products: 58 us -> none  [the longest x4 25.3 us: tile_product(): lax.dot_general(stacked, coupling[1], contract, precision=HIGH, preferred...]
    all_gather x4 -> x0, blocking collectives: 53.7 us -> none  [gathered_by_axis(): nearer = lax.all_gather(value, axes[-1], axis=dim, tiled=True)]
    all_to_all x4 -> x0, starting transfers between devices: 27.7 us -> none  [copy_for_each(): return lax.all_to_all(copies, axis, split_axis=0, concat_axis=0, tiled=True)]
  transfers between devices with their start and end apart: 8 -> 0, of which waited for: 8 -> 0; matrix products, arithmetic and copies ran while one was open for 0% -> 0% of each run, Pallas kernels for 0% -> 0%
where the time goes in v1:
time: 122 us
  Pallas kernels  118 us (97%)
  local copies, waits for them, and re-layouts  3.04 us (2%)
    pallas_call x1, Pallas kernels, body(): pl.pallas_call(kernel, name='subspace', out_shape=(jax.ShapeDtypeStruct((...  118 us
    unnamed x2, local copies, waits for them, and re-layouts  3.04 us

profile of v1, /device:TPU:1, one launch (start us, length us, event | category | flops | bytes accessed | tf_op | source)
XLA Modules:
  0.0 121.6 jit_solution(9734361386719512417)
XLA Ops:
  0.6 117.9 %subspace.1 = (f32[2,48,64]{2,1,0:T(8,128)}, f32[4,2,48,48]{3,2,1,0:T(8,128)}) custom-call(f32[2,512,2048]{2,1,0:T(8,128)} %coupling.1, f32[2,48,512]{2,1,0:T(8,128)} %initial.1), custom_call_target="tpu_custom_call" | custom-call | tf_op jit(solution)/shard_map/subspace/pallas_call | solution.py:547
  118.6 1.4 %copy.6 = f32[2,48,64]{2,1,0:T(8,128)} copy(f32[2,48,64]{2,1,0:T(8,128)} %get-tuple-element.4) | data formatting | bytes 49152
  120.0 1.6 %copy.7 = f32[4,2,48,48]{3,2,1,0:T(8,128)} copy(f32[4,2,48,48]{3,2,1,0:T(8,128)} %get-tuple-element.5) | data formatting | bytes 147456

commit v2 on v1

v2 whole, which is shorter than its diff:
```python
import jax
import jax.numpy as jnp
from jax import lax
from jax.experimental import pallas as pl
from jax.experimental.pallas import tpu as pltpu
from jax.sharding import PartitionSpec as P

N = 16384
K = 48
ITERS = 4
X, Z, C = 4, 8, 8
CH = 256
HALF = K // 2
F32, BF16 = jnp.float32, jnp.bfloat16
MESH = pl.DeviceIdType.MESH
HIGH = lax.Precision.HIGHEST
NT = (((1,), (1,)), ((), ()))


def dot(a, b, precision=None):
    return jnp.dot(a, b, precision=precision, preferred_element_type=F32)


def dot_nt(a, b, precision=None):
    return lax.dot_general(a, b, NT, precision=precision, preferred_element_type=F32)


def split(value):
    high = value.astype(BF16)
    return high, (value - high.astype(F32)).astype(BF16)


def lanes(shape):
    return lax.broadcasted_iota(jnp.int32, shape, 1)


def turned(packed):
    rolled = pltpu.roll(packed, 64, 1)
    return jnp.where(lanes(packed.shape) < 64, rolled, -rolled)


def stacked_rows(first, second):
    gap = jnp.zeros((64 - K, first.shape[1]), first.dtype)
    return jnp.concatenate([first, gap, second, gap], axis=0)


def gram_packed(left, right):
    return dot_nt(left, stacked_rows(right, turned(right)), HIGH)


def gram_planes(re, im):
    return dot_nt(re, stacked_rows(re, im), HIGH) + dot_nt(im, stacked_rows(im, -re), HIGH)


def planes_of(packed):
    low = lanes(packed.shape) < 64
    return jnp.where(low, packed, 0.0), jnp.where(low, pltpu.roll(packed, 64, 1), 0.0)


def apply_packed(matrix, packed):
    re, im = planes_of(matrix)
    return dot(re[:, :K], packed, HIGH) - dot(im[:, :K], turned(packed), HIGH)


def conj_apply_packed(matrix, packed):
    re, im = planes_of(matrix)
    return dot(re[:, :K], packed, HIGH) + dot(im[:, :K], turned(packed), HIGH)


def embedded(matrix, h):
    re, im = planes_of(matrix)
    rows, width = slice(HALF * h, HALF * h + HALF), HALF * (h + 1)
    upper = re[rows] - pltpu.roll(im[rows], width, 1)
    lower = im[rows] + pltpu.roll(re[rows], width, 1)
    return jnp.concatenate([upper, lower], axis=0)[:, : 2 * width]


def inverse_factor(gram):
    lane = lanes((K, 128))
    row = lax.broadcasted_iota(jnp.int32, (K, 128), 0)
    low = lane < 64
    re = jnp.where(low, gram, jnp.where(lane - 64 == row, 1.0, 0.0))
    im = jnp.where(low, pltpu.roll(gram, 64, 1), 0.0)
    done_re, done_im = [], []
    for base in range(0, K, 8):
        below = lax.broadcasted_iota(jnp.int32, (K - base, 1), 0)
        for s in range(8):
            j = base + s
            row_re, row_im = re[s : s + 1], im[s : s + 1]
            inv = 1.0 / re[s : s + 1, j : j + 1]
            m_re = jnp.where(below > s, re[:, j : j + 1] * inv, 0.0)
            m_im = jnp.where(below > s, im[:, j : j + 1] * inv, 0.0)
            re, im = (
                re - (m_re * row_re - m_im * row_im),
                im - (m_re * row_im + m_im * row_re),
            )
        done_re.append(re[:8])
        done_im.append(im[:8])
        re, im = re[8:], im[8:]
    re = jnp.concatenate(done_re, axis=0)
    im = jnp.concatenate(done_im, axis=0)
    pivot = jnp.sum(jnp.where(lane == row, re, 0.0), axis=1, keepdims=True)
    scale = 1.0 / jnp.sqrt(pivot)
    return jnp.where(low, pltpu.roll(re, 64, 1), im) * scale


def pack_pair(re, im):
    low = lanes(re.shape) < 64
    even = jnp.where(low, re, pltpu.roll(im, 64, 1))
    odd = jnp.where(low, pltpu.roll(re, 64, 1), im)
    return even, odd


def unpack_pair(even, odd):
    low = lanes(even.shape) < 64
    re = jnp.where(low, even, pltpu.roll(odd, 64, 1))
    im = jnp.where(low, pltpu.roll(even, 64, 1), odd)
    return re, im


def far_first(k):
    return 4 + (k // 2) * (1 - k % 2) - ((k + 1) // 2) * (k % 2)


def near_first(k):
    return (8 + far_first(7 - k)) % 8


def kernel(coupling, initial, basis, ritz, *scratch):
    (
        stage, hhi, hlo, lhs, part, rsx, red, rsz, gath, ybuf, ysplit, acc, acc2,
        pk, rsy, gy, vpk, scat, ypc, gsrc, gyc, gxs, gx, gzs, gz,
        g4, g4y, g4x, g4z, psrc, py, px, pz, pall,
        hsem, rsx_s, rsx_r, rsz_s, rsz_r, agz_s, agz_r, agx_s, agx_r,
        rsy_s, rsy_r, agy_s, agy_r, sc_s, sc_r, gyc_s, gyc_r, gx_s, gx_r, gz_s, gz_r,
        g4y_s, g4y_r, g4x_s, g4x_r, g4z_s, g4z_r, py_s, py_r, px_s, px_r, pz_s, pz_r, pa_s, pa_r,
    ) = scratch
    r, c = lax.axis_index("rows"), lax.axis_index("cols")
    z, x = r // X, r % X

    def at_x(j):
        return (z * X + (x + j) % X, c)

    def at_z(o):
        return (((z + o) % Z) * X + x, c)

    def at_c(k):
        return (r, (c + k) % C)

    def remote(src, dst, send, recv, dev):
        return pltpu.make_async_remote_copy(
            src_ref=src, dst_ref=dst, send_sem=send, recv_sem=recv,
            device_id=dev, device_id_type=MESH,
        )

    def loop(n, f):
        def step(i, carry):
            f(i)
            return carry

        lax.fori_loop(0, n, step, 0)

    def load(k):
        zc = (z + far_first(k)) % Z
        columns = pl.ds(pl.multiple_of(zc * CH, CH), CH)
        return pltpu.make_async_copy(coupling.at[:, :, columns], stage.at[zc], hsem.at[zc])

    loop(Z, lambda k: load(k).start())

    barrier = pltpu.get_barrier_semaphore()
    partners = [at_x(j) for j in range(1, X)] + [at_z(o) for o in range(1, Z)]
    partners += [at_c(k) for k in range(1, C)]
    for dev in partners:
        pl.semaphore_signal(barrier, inc=1, device_id=dev, device_id_type=MESH)

    def set_left(h, re, im):
        top = jnp.concatenate([re, im], axis=1)
        bottom = jnp.concatenate([im, -re], axis=1)
        high, low = split(jnp.concatenate([top, bottom], axis=0))
        lhs[h] = jnp.concatenate([high, low], axis=0)


    def x_part(h, j, zc):
        return remote(
            part.at[h, zc, (x + j) % X], rsx.at[h, j - 1, zc],
            rsx_s.at[h, j - 1, zc], rsx_r.at[h, j - 1, zc], at_x(j),
        )

    def z_part(h, o, zc):
        return remote(red.at[h, zc], rsz.at[h, o], rsz_s.at[h, o], rsz_r.at[h, o], at_z(o))

    def send_parts(h, zc):
        for j in (2, 1, 3):
            x_part(h, j, zc).start()

    def column_product(h, load_first, send):
        def chunk(k):
            zc = (z + far_first(k)) % Z
            if load_first:
                load(k).wait()
                for t in range(0, 1024, 128):
                    high, low = split(stage[zc, t // 512, t % 512 : t % 512 + 128])
                    hhi[zc, t : t + 128] = high
                    hlo[zc, t : t + 128] = low
            both = dot(lhs[h], hhi[zc])
            total = both[:K] + both[K:] + dot(lhs[h, :K], hlo[zc])
            for q in range(X):
                part[h, zc, q] = total[
                    HALF * (q // 2) : HALF * (q // 2) + HALF, 128 * (q % 2) : 128 * (q % 2) + 128
                ]
            if send:
                send_parts(h, zc)

        loop(Z, chunk)

    def column_sum(h):
        def chunk(k):
            o = far_first(k)
            zc = (z + o) % Z
            total = part[h, zc, x]
            for j in range(1, X):
                x_part(h, j, zc).wait_recv()
                total = total + rsx[h, j - 1, zc]
            red[h, zc] = total

            @pl.when(k < Z - 1)
            def _():
                z_part(h, o, zc).start()

        loop(Z, chunk)

    def sums_sent(h):
        def chunk(k):
            o = far_first(k)
            zc = (z + o) % Z
            for j in range(1, X):
                x_part(h, j, zc).wait_send()
                x_whole(h, j, zc, 0).wait_send()

            @pl.when(k < Z - 1)
            def _():
                z_part(h, o, zc).wait_send()
                z_whole(h, o, z).wait_send()

        loop(Z, chunk)


    def z_whole(h, o, zc):
        piece = gath.at[h, zc, x]
        return remote(piece, piece, agz_s.at[h, o], agz_r.at[h, o], at_z(o))

    def x_whole(h, j, zc, shift):
        piece = gath.at[h, zc, (x + shift) % X]
        return remote(piece, piece, agx_s.at[h, j - 1, zc], agx_r.at[h, j - 1, zc], at_x(j))

    def column_gather(h):
        total = red[h, z]
        for o in range(1, Z):
            z_part(h, o, z).wait_recv()
            total = total + rsz[h, o]
        gath[h, z, x] = total
        loop(Z - 1, lambda k: z_whole(h, far_first(k), z).start())
        for j in range(1, X):
            x_whole(h, j, z, 0).start()

    def column_forward(h):
        def forward(k):
            o = near_first(k + 1)
            zc = (z + Z - o) % Z
            z_whole(h, o, zc).wait_recv()
            for j in (2, 1, 3):
                x_whole(h, j, zc, 0).start()

        loop(Z - 1, forward)

    def column_exchange():
        for h in range(2):
            column_sum(h)
        for h in range(2):
            column_gather(h)
        for h in range(2):
            column_forward(h)

    def c_gram(t, k):
        return remote(gsrc, gyc.at[t, k], gyc_s.at[t, k], gyc_r.at[t, k], at_c(k))

    def c_scatter(t, k):
        return remote(scat.at[t, (c + k) % C], ypc.at[t], sc_s.at[t, k], sc_r.at[t], at_c(k))

    def c_part(h, k):
        return remote(pk.at[h, (c + k) % C], rsy.at[h, k], rsy_s.at[h, k], rsy_r.at[h, k], at_c(k))

    def gathered(h, zc):
        left = jnp.concatenate([gath[h, zc, 0], gath[h, zc, 2]], axis=0)
        right = jnp.concatenate([gath[h, zc, 1], gath[h, zc, 3]], axis=0)
        return jnp.concatenate([left, right], axis=1)

    def row_receive(h, inverse):
        if inverse is not None:
            factor = embedded(inverse, h)

        def receive(k):
            zc = (z + Z - near_first(k)) % Z
            for j in range(1, X):
                x_whole(h, j, zc, X - j).wait_recv()
            block = gathered(h, zc)
            if inverse is not None:
                if h == 1:
                    other = gathered(0, zc)
                    block = jnp.concatenate([other[:HALF], block[:HALF], other[HALF:], block[HALF:]], axis=0)
                block = dot(factor, block, HIGH)
            ybuf[0, zc, HALF * h : HALF * h + HALF] = block[:HALF]
            ybuf[1, zc, HALF * h : HALF * h + HALF] = block[HALF:]
            high, low = split(block)
            ysplit[h, zc] = jnp.concatenate([high, low], axis=0)

        loop(Z, receive)

    def row_gram(t):
        gsrc[...] = lax.fori_loop(
            0, Z, lambda k, gram: gram + gram_planes(ybuf[0, k], ybuf[1, k]), jnp.zeros((K, 128), F32)
        )
        for k in range(1, C):
            c_gram(t, k).start()

        @pl.when(c == z)
        def _():
            for q in range(4):
                part_lanes = slice((q % 2) * 128, (q % 2) * 128 + 128)
                even, odd = pack_pair(
                    ybuf[0, 2 * x + q // 2, :, part_lanes], ybuf[1, 2 * x + q // 2, :, part_lanes]
                )
                scat[t, 2 * q], scat[t, 2 * q + 1] = even, odd
            for k in range(1, C):
                c_scatter(t, k).start()
            ypc[t] = scat[t, c]

    def row_product(h):
        acc[...] = jnp.zeros_like(acc)
        acc2[...] = jnp.zeros_like(acc2)

        def chunk(k):
            acc[...] += dot_nt(ysplit[h, k], hhi[k])
            acc2[...] += dot_nt(ysplit[h, k, :K], hlo[k])

        loop(Z, chunk)
        total = acc[:K] + acc[K:] + acc2[...]
        re = total[:HALF, :512] - total[HALF:, 512:]
        im = total[HALF:, :512] + total[:HALF, 512:]
        for q in range(4):
            even, odd = pack_pair(re[:, 128 * q : 128 * q + 128], im[:, 128 * q : 128 * q + 128])
            pk[h, 2 * q], pk[h, 2 * q + 1] = even, odd
        for k in range(1, C):
            c_part(h, k).start()

    def row_products(t, inverse):
        row_receive(0, inverse)
        row_product(0)
        row_receive(1, inverse)
        row_gram(t)
        row_product(1)

    def row_sum(h):
        total = pk[h, c]
        for k in range(1, C):
            c_part(h, k).wait_recv()
            total = total + rsy[h, k]
        return total

    def c_factor(t):
        total = gsrc[...]
        for k in range(1, C):
            c_gram(t, k).wait_recv()
            total = total + gyc[t, k]
        return inverse_factor(total * (1.0 / N))

    def scattered(t):
        @pl.when(c != z)
        def _():
            c_scatter(t, 1).wait_recv()

        return ypc[t]

    def row_sent(t):
        for k in range(1, C):
            for h in range(2):
                c_part(h, k).wait_send()
            c_gram(t, k).wait_send()

        @pl.when(c == z)
        def _():
            for k in range(1, C):
                c_scatter(t, k).wait_send()

    v_re, v_im = initial[0], initial[1]
    for h in range(2):
        set_left(h, v_re[HALF * h : HALF * h + HALF], v_im[HALF * h : HALF * h + HALF])
    column_product(0, True, False)
    pl.semaphore_wait(barrier, len(partners))
    loop(Z, lambda k: send_parts(0, (z + far_first(k)) % Z))
    column_product(1, False, True)
    for q in range(4):
        even, odd = pack_pair(v_re[:, 128 * q : 128 * q + 128], v_im[:, 128 * q : 128 * q + 128])
        vpk[2 * q], vpk[2 * q + 1] = even, odd
    v_piece = vpk[c]
    column_exchange()
    row_products(0, None)

    def c_whole(h, k, src):
        return remote(gy.at[h, src], gy.at[h, src], agy_s.at[h, k], agy_r.at[h, k], at_c(k))

    z2_piece = []
    for h in range(2):
        z2_piece.append(row_sum(h))
        gy[h, c] = z2_piece[h]
        for k in range(1, C):
            c_whole(h, k, c).start()
    z2_piece = jnp.concatenate(z2_piece, axis=0)
    inv1 = c_factor(0)
    for h in range(2):
        sums_sent(h)
    got_re, got_im, y2_re, y2_im = [], [], [], []
    for h in range(2):
        for k in range(1, C):
            c_whole(h, k, (c + C - k) % C).wait_recv()
        pairs = [unpack_pair(gy[h, 2 * q], gy[h, 2 * q + 1]) for q in range(4)]
        got_re.append(jnp.concatenate([pair[0] for pair in pairs], axis=1))
        got_im.append(jnp.concatenate([pair[1] for pair in pairs], axis=1))
        block = dot(embedded(inv1, h), jnp.concatenate(got_re + got_im, axis=0), HIGH)
        y2_re.append(block[:HALF])
        y2_im.append(block[HALF:])
        set_left(h, block[:HALF], block[HALF:])
        column_product(h, False, True)
    gxs[...] = gram_planes(jnp.concatenate(y2_re, axis=0), jnp.concatenate(y2_im, axis=0))

    def x_gram(j):
        return remote(gxs, gx.at[j], gx_s.at[j], gx_r.at[j], at_x(j))

    def z_gram(o):
        return remote(gzs, gz.at[o], gz_s.at[o], gz_r.at[o], at_z(o))

    for j in range(1, X):
        x_gram(j).start()
    row_sent(0)
    y2_piece = apply_packed(inv1, z2_piece)
    y1_piece = scattered(0)
    psrc[:K] = gram_packed(v_piece, y1_piece)
    psrc[K : 2 * K] = conj_apply_packed(inv1, gram_packed(y1_piece, y2_piece))
    for h in range(2):
        column_sum(h)
    total = gxs[...]
    for j in range(1, X):
        x_gram(j).wait_recv()
        total = total + gx[j]
    gzs[...] = total
    for o in range(1, Z):
        z_gram(o).start()
    for h in range(2):
        column_gather(h)
    for h in range(2):
        column_forward(h)
    total = gzs[...]
    for o in range(1, Z):
        z_gram(o).wait_recv()
        total = total + gz[o]
    inv2 = inverse_factor(total * (1.0 / N))
    row_products(1, inv2)
    inv3 = c_factor(1)
    y4_piece = apply_packed(inv3, jnp.concatenate([row_sum(0), row_sum(1)], axis=0))


    def g_c(k):
        return remote(g4.at[0], g4y.at[k], g4y_s.at[k], g4y_r.at[k], at_c(k))

    def g_x(j):
        return remote(g4.at[1], g4x.at[j], g4x_s.at[j], g4x_r.at[j], at_x(j))

    def g_z(o):
        return remote(g4.at[2], g4z.at[o], g4z_s.at[o], g4z_r.at[o], at_z(o))

    def slab(shift):
        return pl.ds(pl.multiple_of(((c + shift) % C) * HALF, 8), HALF)

    def p_c(k):
        return remote(psrc.at[slab(k)], py.at[k], py_s.at[k], py_r.at[k], at_c(k))

    def p_x(j):
        return remote(px.at[0], px.at[j], px_s.at[j], px_r.at[j], at_x(j))

    def p_z(o):
        return remote(pz.at[0], pz.at[o], pz_s.at[o], pz_r.at[o], at_z(o))

    def p_all(k, shift):
        return remote(pall.at[slab(shift)], pall.at[slab(shift)], pa_s.at[k], pa_r.at[k], at_c(k))

    def added(total, n, copy, slots):
        for i in range(1, n):
            copy(i).wait_recv()
            total = total + slots[i]
        return total

    gram = gram_packed(y4_piece, y4_piece)
    g4[0] = gram
    for k in range(1, C):
        g_c(k).start()
    y3_piece = scattered(1)
    psrc[2 * K : 3 * K] = conj_apply_packed(inv2, gram_packed(y2_piece, y3_piece))
    psrc[3 * K :] = conj_apply_packed(inv3, gram_packed(y3_piece, y4_piece))
    for k in range(1, C):
        p_c(k).start()
    gram = added(gram, C, g_c, g4y)
    g4[1] = gram
    for j in range(1, X):
        g_x(j).start()
    px[0] = added(psrc[slab(0)], C, p_c, py)
    for j in range(1, X):
        p_x(j).start()
    gram = added(gram, X, g_x, g4x)
    g4[2] = gram
    for o in range(1, Z):
        g_z(o).start()
    pz[0] = added(px[0], X, p_x, px)
    for o in range(1, Z):
        p_z(o).start()
    gram = added(gram, Z, g_z, g4z)
    pall[slab(0)] = added(pz[0], Z, p_z, pz) * (1.0 / N)
    for k in range(1, C):
        p_all(k, 0).start()
    value = apply_packed(inverse_factor(gram * (1.0 / N)), y4_piece)
    basis[0] = value[:, :64]
    basis[1] = pltpu.roll(value, 64, 1)[:, :64]
    for k in range(1, C):
        p_all(k, C - k).wait_recv()
    for t in range(ITERS):
        value = pall[K * t : K * t + K]
        ritz[t, 0] = value[:, :K]
        ritz[t, 1] = pltpu.roll(value, 64, 1)[:, :K]

    for h in range(2):
        sums_sent(h)
        for k in range(1, C):
            c_whole(h, k, c).wait_send()
    row_sent(1)
    for k in range(1, C):
        g_c(k).wait_send()
        p_c(k).wait_send()
        p_all(k, 0).wait_send()
    for j in range(1, X):
        x_gram(j).wait_send()
        g_x(j).wait_send()
        p_x(j).wait_send()
    for o in range(1, Z):
        z_gram(o).wait_send()
        g_z(o).wait_send()
        p_z(o).wait_send()


def solution(mesh):
    dma = pltpu.SemaphoreType.DMA
    packed, piece = (K, 128), (HALF, 128)
    scratch = [
        pltpu.VMEM((Z, 2, 512, CH), F32),
        pltpu.VMEM((Z, 1024, CH), BF16),
        pltpu.VMEM((Z, 1024, CH), BF16),
        pltpu.VMEM((2, 2 * K, 1024), BF16),
        pltpu.VMEM((2, Z, X, *piece), F32),
        pltpu.VMEM((2, X - 1, Z, *piece), F32),
        pltpu.VMEM((2, Z, *piece), F32),
        pltpu.VMEM((2, Z, *piece), F32),
        pltpu.VMEM((2, Z, X, *piece), F32),
        pltpu.VMEM((2, Z, K, CH), F32),
        pltpu.VMEM((2, Z, 2 * K, CH), BF16),
        pltpu.VMEM((2 * K, 1024), F32),
        pltpu.VMEM((K, 1024), F32),
        pltpu.VMEM((2, C, *piece), F32),
        pltpu.VMEM((2, C, *piece), F32),
        pltpu.VMEM((2, C, *piece), F32),
        pltpu.VMEM((C, *packed), F32),
        pltpu.VMEM((2, C, *packed), F32),
        pltpu.VMEM((2, *packed), F32),
        pltpu.VMEM(packed, F32),
        pltpu.VMEM((2, C, *packed), F32),
        pltpu.VMEM(packed, F32),
        pltpu.VMEM((X, *packed), F32),
        pltpu.VMEM(packed, F32),
        pltpu.VMEM((Z, *packed), F32),
        pltpu.VMEM((3, *packed), F32),
        pltpu.VMEM((C, *packed), F32),
        pltpu.VMEM((X, *packed), F32),
        pltpu.VMEM((Z, *packed), F32),
        pltpu.VMEM((4 * K, 128), F32),
        pltpu.VMEM((C, *piece), F32),
        pltpu.VMEM((X, *piece), F32),
        pltpu.VMEM((Z, *piece), F32),
        pltpu.VMEM((4 * K, 128), F32),
        dma((Z,)),
        dma((2, X - 1, Z)), dma((2, X - 1, Z)), dma((2, Z)), dma((2, Z)),
        dma((2, Z)), dma((2, Z)), dma((2, X - 1, Z)), dma((2, X - 1, Z)),
        dma((2, C)), dma((2, C)), dma((2, C)), dma((2, C)),
        dma((2, C)), dma((2,)), dma((2, C)), dma((2, C)),
        dma((X,)), dma((X,)), dma((Z,)), dma((Z,)),
        dma((C,)), dma((C,)), dma((X,)), dma((X,)), dma((Z,)), dma((Z,)),
        dma((C,)), dma((C,)), dma((X,)), dma((X,)), dma((Z,)), dma((Z,)), dma((C,)), dma((C,)),
    ]
    vmem = pl.BlockSpec(memory_space=pltpu.VMEM)

    def body(coupling, initial):
        return pl.pallas_call(
            kernel,
            name="subspace",
            out_shape=(
                jax.ShapeDtypeStruct((2, K, 64), F32),
                jax.ShapeDtypeStruct((ITERS, 2, K, K), F32),
            ),
            in_specs=[pl.BlockSpec(memory_space=pl.ANY), vmem],
            out_specs=(vmem, vmem),
            scratch_shapes=scratch,
            compiler_params=pltpu.CompilerParams(
                collective_id=0, has_side_effects=True, vmem_limit_bytes=56 * 1024 * 1024
            ),
        )(coupling, initial)

    return jax.shard_map(
        body,
        mesh=mesh,
        in_specs=(P(None, "rows", "cols"), P(None, None, "rows")),
        out_specs=(P(None, None, ("rows", "cols")), P()),
        check_vma=False,
    )
```

time: 122 us -> 136 us (1.11)
  Pallas kernels: 118 us -> 132 us
    pallas_call x1, Pallas kernels: 118 us -> 132 us  [body(): pl.pallas_call(kernel, name='subspace', out_shape=(jax.ShapeDtypeStruct((...]
where the time goes in v2:
time: 136 us
  Pallas kernels  132 us (97%)
  local copies, waits for them, and re-layouts  3.04 us (2%)
    pallas_call x1, Pallas kernels, body(): pl.pallas_call(kernel, name='subspace', out_shape=(jax.ShapeDtypeStruct((...  132 us
    unnamed x2, local copies, waits for them, and re-layouts  3.04 us

profile of v2, /device:TPU:1, one launch (start us, length us, event | category | flops | bytes accessed | tf_op | source)
XLA Modules:
  0.0 135.8 jit_solution(6185416845930021998)
XLA Ops:
  0.6 132.1 %subspace.1 = (f32[2,48,64]{2,1,0:T(8,128)}, f32[4,2,48,48]{3,2,1,0:T(8,128)}) custom-call(f32[2,512,2048]{2,1,0:T(8,128)} %coupling.1, f32[2,48,512]{2,1,0:T(8,128)} %initial.1), custom_call_target="tpu_custom_call" | custom-call | tf_op jit(solution)/shard_map/subspace/pallas_call | solution.py:608
  132.7 1.4 %copy.6 = f32[2,48,64]{2,1,0:T(8,128)} copy(f32[2,48,64]{2,1,0:T(8,128)} %get-tuple-element.4) | data formatting | bytes 49152
  134.2 1.6 %copy.7 = f32[4,2,48,48]{3,2,1,0:T(8,128)} copy(f32[4,2,48,48]{3,2,1,0:T(8,128)} %get-tuple-element.5) | data formatting | bytes 147456

commit v3 on v2

v3 whole, which is shorter than its diff:
```python
import jax
import jax.numpy as jnp
from jax import lax
from jax.experimental import pallas as pl
from jax.experimental.pallas import tpu as pltpu
from jax.sharding import PartitionSpec as P

N = 16384
K = 48
ITERS = 4
X, Z, C = 4, 8, 8
CH = 256
RB = 2 * K // X
F32, BF16 = jnp.float32, jnp.bfloat16
MESH = pl.DeviceIdType.MESH
HIGH = lax.Precision.HIGHEST
NT = (((1,), (1,)), ((), ()))


def dot(a, b, precision=None):
    return jnp.dot(a, b, precision=precision, preferred_element_type=F32)


def dot_nt(a, b, precision=None):
    return lax.dot_general(a, b, NT, precision=precision, preferred_element_type=F32)


def split(value):
    high = value.astype(BF16)
    return high, (value - high.astype(F32)).astype(BF16)


def lanes(shape):
    return lax.broadcasted_iota(jnp.int32, shape, 1)


def turned(packed):
    rolled = pltpu.roll(packed, 64, 1)
    return jnp.where(lanes(packed.shape) < 64, rolled, -rolled)


def stacked_rows(first, second):
    gap = jnp.zeros((64 - K, first.shape[1]), first.dtype)
    return jnp.concatenate([first, gap, second, gap], axis=0)


def gram_packed(left, right):
    return dot_nt(left, stacked_rows(right, turned(right)), HIGH)


def gram_planes(re, im):
    return dot_nt(re, stacked_rows(re, im), HIGH) + dot_nt(im, stacked_rows(im, -re), HIGH)


def planes_of(packed):
    low = lanes(packed.shape) < 64
    return jnp.where(low, packed, 0.0), jnp.where(low, pltpu.roll(packed, 64, 1), 0.0)


def apply_packed(matrix, packed):
    re, im = planes_of(matrix)
    return dot(re[:, :K], packed, HIGH) - dot(im[:, :K], turned(packed), HIGH)


def conj_apply_packed(matrix, packed):
    re, im = planes_of(matrix)
    return dot(re[:, :K], packed, HIGH) + dot(im[:, :K], turned(packed), HIGH)


def embedded(matrix):
    re, im = planes_of(matrix)
    upper = re - pltpu.roll(im, K, 1)
    lower = im + pltpu.roll(re, K, 1)
    return jnp.concatenate([upper, lower], axis=0)[:, : 2 * K]


def factor_steps(gram, result):
    lane = lanes((K, 128))
    row = lax.broadcasted_iota(jnp.int32, (K, 128), 0)
    low = lane < 64
    re = jnp.where(low, gram, jnp.where(lane - 64 == row, 1.0, 0.0))
    im = jnp.where(low, pltpu.roll(gram, 64, 1), 0.0)
    done_re, done_im = [], []
    for base in range(0, K, 8):
        below = lax.broadcasted_iota(jnp.int32, (K - base, 1), 0)
        for s in range(8):
            j = base + s
            row_re, row_im = re[s : s + 1], im[s : s + 1]
            inv = 1.0 / re[s : s + 1, j : j + 1]
            m_re = jnp.where(below > s, re[:, j : j + 1] * inv, 0.0)
            m_im = jnp.where(below > s, im[:, j : j + 1] * inv, 0.0)
            re, im = (
                re - (m_re * row_re - m_im * row_im),
                im - (m_re * row_im + m_im * row_re),
            )
        done_re.append(re[:8])
        done_im.append(im[:8])
        re, im = re[8:], im[8:]
        yield
    re = jnp.concatenate(done_re, axis=0)
    im = jnp.concatenate(done_im, axis=0)
    pivot = jnp.sum(jnp.where(lane == row, re, 0.0), axis=1, keepdims=True)
    scale = 1.0 / jnp.sqrt(pivot)
    result.append(jnp.where(low, pltpu.roll(re, 64, 1), im) * scale)


def inverse_factor(gram):
    result = []
    for _ in factor_steps(gram, result):
        pass
    return result[0]


def both_sides(matrix, packed):
    left = conj_apply_packed(matrix, packed)
    low = lanes(matrix.shape) < 64
    return dot_nt(left, stacked_rows(jnp.where(low, matrix, -matrix), pltpu.roll(matrix, 64, 1)), HIGH)


def pack_pair(re, im):
    low = lanes(re.shape) < 64
    even = jnp.where(low, re, pltpu.roll(im, 64, 1))
    odd = jnp.where(low, pltpu.roll(re, 64, 1), im)
    return even, odd


def unpack_pair(even, odd):
    low = lanes(even.shape) < 64
    re = jnp.where(low, even, pltpu.roll(odd, 64, 1))
    im = jnp.where(low, pltpu.roll(even, 64, 1), odd)
    return re, im


def far_first(k):
    return 4 + (k >> 1) * (1 - (k & 1)) - ((k + 1) >> 1) * (k & 1)


def near_first(k):
    return far_first(7 - k) & 7


def kernel(coupling, initial, basis, ritz, *scratch):
    (
        stage, hhi, hlo, lhs, part, rsx, mixed, red, rsz, gath, ybuf, acc, acc2,
        pk, rsy, gy, scat, ypc, gsrc, gyc, gxs, gx, gzs, gz,
        g4, g4y, g4x, g4z, psrc, py, px, pz, pall,
        hsem, rsx_s, rsx_r, rsz_s, rsz_r, agz_s, agz_r, agx_s, agx_r,
        rsy_s, rsy_r, agy_s, agy_r, sc_s, sc_r, gyc_s, gyc_r, gx_s, gx_r, gz_s, gz_r,
        g4y_s, g4y_r, g4x_s, g4x_r, g4z_s, g4z_r, py_s, py_r, px_s, px_r, pz_s, pz_r, pa_s, pa_r,
    ) = scratch
    r, c = lax.axis_index("rows"), lax.axis_index("cols")
    z, x = r >> 2, r & 3

    def at_x(j):
        return (z * X + ((x + j) & 3), c)

    def at_z(o):
        return (((z + o) & 7) * X + x, c)

    def at_c(k):
        return (r, (c + k) & 7)

    def remote(src, dst, send, recv, dev):
        return pltpu.make_async_remote_copy(
            src_ref=src, dst_ref=dst, send_sem=send, recv_sem=recv,
            device_id=dev, device_id_type=MESH,
        )

    def loop(n, f):
        def step(i, carry):
            f(i)
            return carry

        lax.fori_loop(0, n, step, 0)

    def rows_of(j):
        return pl.ds(pl.multiple_of(((x + j) & 3) * RB, 8), RB)

    def far(k):
        return (z + far_first(k)) & 7

    def near(k):
        return (z + 8 - near_first(k)) & 7

    def side(k):
        return 1 - 2 * (k & 1)

    def load(k):
        columns = pl.ds(pl.multiple_of(far(k) * CH, CH), CH)
        return pltpu.make_async_copy(coupling.at[:, :, columns], stage.at[far(k)], hsem.at[far(k)])

    loop(Z, lambda k: load(k).start())

    barrier = pltpu.get_barrier_semaphore()
    partners = [at_x(j) for j in range(1, X)] + [at_z(o) for o in range(1, Z)]
    partners += [at_c(k) for k in range(1, C)]
    for dev in partners:
        pl.semaphore_signal(barrier, inc=1, device_id=dev, device_id_type=MESH)

    def set_left(re, im):
        top = jnp.concatenate([re, im], axis=1)
        bottom = jnp.concatenate([im, -re], axis=1)
        high, low = split(jnp.concatenate([top, bottom], axis=0))
        lhs[...] = jnp.concatenate([high, low], axis=0)


    def x_part(k, which):
        zc, s = far(k), side(k)
        source = [part.at[zc, rows_of(2)], part.at[zc, rows_of(-s)], mixed.at[zc]][which]
        return remote(
            source, rsx.at[which, zc], rsx_s.at[which, zc], rsx_r.at[which, zc], at_x([s, -s, s][which])
        )

    def z_part(k):
        o = far_first(k)
        return remote(red.at[far(k)], rsz.at[o], rsz_s.at[o], rsz_r.at[o], at_z(o))

    def send_parts(k):
        x_part(k, 0).start()
        x_part(k, 1).start()

    def column_product(load_first, send):
        def chunk(k):
            zc = far(k)
            if load_first:
                load(k).wait()
                for t in range(0, 1024, 128):
                    high, low = split(stage[zc, t // 512, t % 512 : t % 512 + 128])
                    hhi[zc, t : t + 128] = high
                    hlo[zc, t : t + 128] = low
            both = dot(lhs[...], hhi[zc])
            part[zc] = both[: 2 * K] + both[2 * K :] + dot(lhs[: 2 * K], hlo[zc])
            if send:
                send_parts(k)

        loop(Z, chunk)

    def column_mix():
        def chunk(k):
            x_part(k, 0).wait_recv()
            mixed[far(k)] = part[far(k), rows_of(side(k))] + rsx[0, far(k)]
            x_part(k, 2).start()

        loop(Z, chunk)

    def column_sum():
        def chunk(k):
            zc = far(k)
            x_part(k, 1).wait_recv()
            x_part(k, 2).wait_recv()
            red[zc] = part[zc, rows_of(0)] + rsx[1, zc] + rsx[2, zc]

            @pl.when(k < Z - 1)
            def _():
                z_part(k).start()

        loop(Z, chunk)


    def z_whole(o, zc):
        block = gath.at[zc, rows_of(0)]
        return remote(block, block, agz_s.at[o], agz_r.at[o], at_z(o))

    def x_whole(k, which, sent=True):
        zc, s = near(k), side(k)
        straight = k >= Z - 2
        shift = 0 if sent and (which < 2 or straight) else (-s if sent else [-s, s, 2][which])
        block = gath.at[zc, rows_of(shift)]
        dev = at_x([s, -s, 2 if straight else s][which])
        return remote(block, block, agx_s.at[which, k], agx_r.at[which, k], dev)

    def column_gather(steps):
        total = red[z]
        for k in range(Z - 1):
            z_part(k).wait_recv()
            total = total + rsz[far_first(k)]
        gath[z, rows_of(0)] = total
        for k in range(Z - 1):
            z_whole(far_first(k), z).start()

        def pass_on(k):
            x_whole(k, 0, False).wait_recv()
            x_whole(k, 2).start()

        for k in range(Z):
            if k > 0:
                z_whole(near_first(k), near(k)).wait_recv()
            x_whole(k, 0).start()
            x_whole(k, 1).start()
            if k >= Z - 2:
                x_whole(k, 2).start()
            if k >= 2:
                pass_on(k - 2)
            next(steps, None)
        for _ in steps:
            pass

    def column_sent():
        for k in range(Z):
            for which in range(3):
                x_part(k, which).wait_send()
                x_whole(k, which).wait_send()
            if k < Z - 1:
                z_part(k).wait_send()
                z_whole(far_first(k), z).wait_send()

    def c_gram(t, k):
        return remote(gsrc, gyc.at[t, k], gyc_s.at[t, k], gyc_r.at[t, k], at_c(k))

    def c_scatter(t, k):
        return remote(scat.at[t, (c + k) & 7], ypc.at[t], sc_s.at[t, k], sc_r.at[t], at_c(k))

    def c_part(k):
        return remote(pk.at[(c + k) & 7], rsy.at[k], rsy_s.at[k], rsy_r.at[k], at_c(k))

    def row_product(t, factor):
        acc[...] = jnp.zeros_like(acc)
        acc2[...] = jnp.zeros_like(acc2)
        gsrc[...] = jnp.zeros_like(gsrc)
        for k in range(Z):
            zc = near(k)
            if k < Z - 2:
                x_whole(k, 1, False).wait_recv()
                x_whole(k, 2, False).wait_recv()
            else:
                for which in range(3):
                    x_whole(k, which, False).wait_recv()
            block = gath[zc]
            if factor is not None:
                block = dot(factor, block, HIGH)
            ybuf[zc] = block
            high, low = split(block)
            acc[...] += dot_nt(jnp.concatenate([high, low], axis=0), hhi[zc])
            acc2[...] += dot_nt(high, hlo[zc])
            gsrc[...] += gram_planes(block[:K], block[K:])
        for k in range(1, C):
            c_gram(t, k).start()
        total = acc[: 2 * K] + acc[2 * K :] + acc2[...]
        re = total[:K, :512] - total[K:, 512:]
        im = total[K:, :512] + total[:K, 512:]
        for q in range(4):
            even, odd = pack_pair(re[:, 128 * q : 128 * q + 128], im[:, 128 * q : 128 * q + 128])
            pk[2 * q], pk[2 * q + 1] = even, odd
        for k in range(1, C):
            c_part(k).start()

        @pl.when(c == z)
        def _():
            for q in range(4):
                chunk = ybuf.at[2 * x + q // 2]
                part_lanes = slice((q % 2) * 128, (q % 2) * 128 + 128)
                even, odd = pack_pair(chunk[:K, part_lanes], chunk[K:, part_lanes])
                scat[t, 2 * q], scat[t, 2 * q + 1] = even, odd
            for k in range(1, C):
                c_scatter(t, k).start()
            ypc[t] = scat[t, c]

    def row_sum():
        total = pk[c]
        for k in range(1, C):
            c_part(k).wait_recv()
            total = total + rsy[k]
        return total

    def c_factor(t):
        total = gsrc[...]
        for k in range(1, C):
            c_gram(t, k).wait_recv()
            total = total + gyc[t, k]
        return inverse_factor(total * (1.0 / N))

    def scattered(t):
        @pl.when(c != z)
        def _():
            c_scatter(t, 1).wait_recv()

        return ypc[t]

    def row_sent(t):
        for k in range(1, C):
            c_part(k).wait_send()
            c_gram(t, k).wait_send()

        @pl.when(c == z)
        def _():
            for k in range(1, C):
                c_scatter(t, k).wait_send()

    v_re, v_im = initial[0], initial[1]
    set_left(v_re, v_im)
    column_product(True, False)
    pl.semaphore_wait(barrier, len(partners))
    loop(Z, send_parts)
    for q in range(4):
        even, odd = pack_pair(v_re[:, 128 * q : 128 * q + 128], v_im[:, 128 * q : 128 * q + 128])
        pk[2 * q], pk[2 * q + 1] = even, odd
    v_piece = pk[c]
    column_mix()
    column_sum()
    column_gather(iter(()))
    row_product(0, None)
    z2_piece = row_sum()
    gy[c] = z2_piece

    def c_whole(k, src):
        return remote(gy.at[src], gy.at[src], agy_s.at[k], agy_r.at[k], at_c(k))

    for k in range(1, C):
        c_whole(k, c).start()
    inv1 = c_factor(0)
    column_sent()
    for k in range(1, C):
        c_whole(k, (c + C - k) & 7).wait_recv()
    pairs = [unpack_pair(gy[2 * q], gy[2 * q + 1]) for q in range(4)]
    block = jnp.concatenate(
        [jnp.concatenate([pair[p] for pair in pairs], axis=1) for p in range(2)], axis=0
    )
    block = dot(embedded(inv1), block, HIGH)
    set_left(block[:K], block[K:])
    column_product(False, True)
    gxs[...] = gram_planes(block[:K], block[K:])

    def x_gram(j):
        return remote(gxs, gx.at[j], gx_s.at[j], gx_r.at[j], at_x(j))

    def z_gram(o):
        return remote(gzs, gz.at[o], gz_s.at[o], gz_r.at[o], at_z(o))

    for j in range(1, X):
        x_gram(j).start()
    column_mix()
    row_sent(0)
    y2_piece = apply_packed(inv1, z2_piece)
    y1_piece = scattered(0)
    psrc[:K] = gram_packed(v_piece, y1_piece)
    psrc[K : 2 * K] = conj_apply_packed(inv1, gram_packed(y1_piece, y2_piece))
    total = gxs[...]
    for j in range(1, X):
        x_gram(j).wait_recv()
        total = total + gx[j]
    gzs[...] = total
    for o in range(1, Z):
        z_gram(o).start()
    column_sum()
    total = gzs[...]
    for o in range(1, Z):
        z_gram(o).wait_recv()
        total = total + gz[o]
    inv2 = []
    column_gather(factor_steps(total * (1.0 / N), inv2))
    inv2 = inv2[0]
    row_product(1, embedded(inv2))
    z4_piece = row_sum()


    def g_c(k):
        return remote(g4.at[0], g4y.at[k], g4y_s.at[k], g4y_r.at[k], at_c(k))

    def g_x(j):
        return remote(g4.at[1], g4x.at[j], g4x_s.at[j], g4x_r.at[j], at_x(j))

    def g_z(o):
        return remote(g4.at[2], g4z.at[o], g4z_s.at[o], g4z_r.at[o], at_z(o))

    def slab(shift):
        return pl.ds(pl.multiple_of(((c + shift) & 7) * RB, 8), RB)

    def p_c(k):
        return remote(psrc.at[slab(k)], py.at[k], py_s.at[k], py_r.at[k], at_c(k))

    def p_x(j):
        return remote(px.at[0], px.at[j], px_s.at[j], px_r.at[j], at_x(j))

    def p_z(o):
        return remote(pz.at[0], pz.at[o], pz_s.at[o], pz_r.at[o], at_z(o))

    def p_all(k, shift):
        return remote(pall.at[slab(shift)], pall.at[slab(shift)], pa_s.at[k], pa_r.at[k], at_c(k))

    def added(total, n, copy, slots):
        for i in range(1, n):
            copy(i).wait_recv()
            total = total + slots[i]
        return total

    gram = gram_packed(z4_piece, z4_piece)
    g4[0] = gram
    for k in range(1, C):
        g_c(k).start()
    inv3 = c_factor(1)
    gram = both_sides(inv3, added(gram, C, g_c, g4y))
    g4[1] = gram
    for j in range(1, X):
        g_x(j).start()
    y4_piece = apply_packed(inv3, z4_piece)
    y3_piece = scattered(1)
    psrc[2 * K : 3 * K] = conj_apply_packed(inv2, gram_packed(y2_piece, y3_piece))
    psrc[3 * K :] = conj_apply_packed(inv3, gram_packed(y3_piece, y4_piece))
    for k in range(1, C):
        p_c(k).start()
    gram = added(gram, X, g_x, g4x)
    g4[2] = gram
    for o in range(1, Z):
        g_z(o).start()
    px[0] = added(psrc[slab(0)], C, p_c, py)
    for j in range(1, X):
        p_x(j).start()
    pz[0] = added(px[0], X, p_x, px)
    for o in range(1, Z):
        p_z(o).start()
    gram = added(gram, Z, g_z, g4z)
    value = []
    steps = factor_steps(gram * (1.0 / N), value)
    for _ in range(3):
        next(steps)
    pall[slab(0)] = added(pz[0], Z, p_z, pz) * (1.0 / N)
    for k in range(1, C):
        p_all(k, 0).start()
    for _ in steps:
        pass
    value = apply_packed(value[0], y4_piece)
    basis[0] = value[:, :64]
    basis[1] = pltpu.roll(value, 64, 1)[:, :64]
    for k in range(1, C):
        p_all(k, C - k).wait_recv()
    for t in range(ITERS):
        value = pall[K * t : K * t + K]
        ritz[t, 0] = value[:, :K]
        ritz[t, 1] = pltpu.roll(value, 64, 1)[:, :K]

    column_sent()
    row_sent(1)
    for k in range(1, C):
        c_whole(k, c).wait_send()
        g_c(k).wait_send()
        p_c(k).wait_send()
        p_all(k, 0).wait_send()
    for j in range(1, X):
        x_gram(j).wait_send()
        g_x(j).wait_send()
        p_x(j).wait_send()
    for o in range(1, Z):
        z_gram(o).wait_send()
        g_z(o).wait_send()
        p_z(o).wait_send()


def solution(mesh):
    dma = pltpu.SemaphoreType.DMA
    packed, piece = (K, 128), (RB, 128)
    scratch = [
        pltpu.VMEM((Z, 2, 512, CH), F32),
        pltpu.VMEM((Z, 1024, CH), BF16),
        pltpu.VMEM((Z, 1024, CH), BF16),
        pltpu.VMEM((4 * K, 1024), BF16),
        pltpu.VMEM((Z, 2 * K, CH), F32),
        pltpu.VMEM((3, Z, RB, CH), F32),
        pltpu.VMEM((Z, RB, CH), F32),
        pltpu.VMEM((Z, RB, CH), F32),
        pltpu.VMEM((Z, RB, CH), F32),
        pltpu.VMEM((Z, 2 * K, CH), F32),
        pltpu.VMEM((Z, 2 * K, CH), F32),
        pltpu.VMEM((4 * K, 1024), F32),
        pltpu.VMEM((2 * K, 1024), F32),
        pltpu.VMEM((C, *packed), F32),
        pltpu.VMEM((C, *packed), F32),
        pltpu.VMEM((C, *packed), F32),
        pltpu.VMEM((2, C, *packed), F32),
        pltpu.VMEM((2, *packed), F32),
        pltpu.VMEM(packed, F32),
        pltpu.VMEM((2, C, *packed), F32),
        pltpu.VMEM(packed, F32),
        pltpu.VMEM((X, *packed), F32),
        pltpu.VMEM(packed, F32),
        pltpu.VMEM((Z, *packed), F32),
        pltpu.VMEM((3, *packed), F32),
        pltpu.VMEM((C, *packed), F32),
        pltpu.VMEM((X, *packed), F32),
        pltpu.VMEM((Z, *packed), F32),
        pltpu.VMEM((4 * K, 128), F32),
        pltpu.VMEM((C, *piece), F32),
        pltpu.VMEM((X, *piece), F32),
        pltpu.VMEM((Z, *piece), F32),
        pltpu.VMEM((4 * K, 128), F32),
        dma((Z,)),
        dma((3, Z)), dma((3, Z)), dma((Z,)), dma((Z,)),
        dma((Z,)), dma((Z,)), dma((3, Z)), dma((3, Z)),
        dma((C,)), dma((C,)), dma((C,)), dma((C,)),
        dma((2, C)), dma((2,)), dma((2, C)), dma((2, C)),
        dma((X,)), dma((X,)), dma((Z,)), dma((Z,)),
        dma((C,)), dma((C,)), dma((X,)), dma((X,)), dma((Z,)), dma((Z,)),
        dma((C,)), dma((C,)), dma((X,)), dma((X,)), dma((Z,)), dma((Z,)), dma((C,)), dma((C,)),
    ]
    vmem = pl.BlockSpec(memory_space=pltpu.VMEM)

    def body(coupling, initial):
        return pl.pallas_call(
            kernel,
            name="subspace",
            out_shape=(
                jax.ShapeDtypeStruct((2, K, 64), F32),
                jax.ShapeDtypeStruct((ITERS, 2, K, K), F32),
            ),
            in_specs=[pl.BlockSpec(memory_space=pl.ANY), vmem],
            out_specs=(vmem, vmem),
            scratch_shapes=scratch,
            compiler_params=pltpu.CompilerParams(
                collective_id=0, has_side_effects=True, vmem_limit_bytes=56 * 1024 * 1024
            ),
        )(coupling, initial)

    return jax.shard_map(
        body,
        mesh=mesh,
        in_specs=(P(None, "rows", "cols"), P(None, None, "rows")),
        out_specs=(P(None, None, ("rows", "cols")), P()),
        check_vma=False,
    )
```

time: 136 us -> 132 us (0.971)
  Pallas kernels: 132 us -> 128 us
    pallas_call x1, Pallas kernels: 132 us -> 128 us  [body(): pl.pallas_call(kernel, name='subspace', out_shape=(jax.ShapeDtypeStruct((...]
where the time goes in v3:
time: 132 us
  Pallas kernels  128 us (97%)
  local copies, waits for them, and re-layouts  3.04 us (2%)
    pallas_call x1, Pallas kernels, body(): pl.pallas_call(kernel, name='subspace', out_shape=(jax.ShapeDtypeStruct((...  128 us
    unnamed x2, local copies, waits for them, and re-layouts  3.04 us

profile of v3, /device:TPU:1, one launch (start us, length us, event | category | flops | bytes accessed | tf_op | source)
XLA Modules:
  0.0 132.1 jit_solution(15205354462071416158)
XLA Ops:
  0.6 128.5 %subspace.1 = (f32[2,48,64]{2,1,0:T(8,128)}, f32[4,2,48,48]{3,2,1,0:T(8,128)}) custom-call(f32[2,512,2048]{2,1,0:T(8,128)} %coupling.1, f32[2,48,512]{2,1,0:T(8,128)} %initial.1), custom_call_target="tpu_custom_call" | custom-call | tf_op jit(solution)/shard_map/subspace/pallas_call | solution.py:597
  129.1 1.4 %copy.6 = f32[2,48,64]{2,1,0:T(8,128)} copy(f32[2,48,64]{2,1,0:T(8,128)} %get-tuple-element.4) | data formatting | bytes 49152
  130.5 1.6 %copy.7 = f32[4,2,48,48]{3,2,1,0:T(8,128)} copy(f32[4,2,48,48]{3,2,1,0:T(8,128)} %get-tuple-element.5) | data formatting | bytes 147456

commit v4 on v3

--- a/solution.py
+++ b/solution.py
@@ -13,16 +13,15 @@
 RB = 2 * K // X
 F32, BF16 = jnp.float32, jnp.bfloat16
 MESH = pl.DeviceIdType.MESH
-HIGH = lax.Precision.HIGHEST
 NT = (((1,), (1,)), ((), ()))
 
 
-def dot(a, b, precision=None):
-    return jnp.dot(a, b, precision=precision, preferred_element_type=F32)
-
-
-def dot_nt(a, b, precision=None):
-    return lax.dot_general(a, b, NT, precision=precision, preferred_element_type=F32)
+def dot(a, b):
+    return jnp.dot(a, b, preferred_element_type=F32)
+
+
+def dot_nt(a, b):
+    return lax.dot_general(a, b, NT, preferred_element_type=F32)
 
 
 def split(value):
@@ -30,6 +29,11 @@
     return high, (value - high.astype(F32)).astype(BF16)
 
 
+def in_parts(product, a, b):
+    (ah, al), (bh, bl) = split(a), split(b)
+    return product(ah, bh) + (product(ah, bl) + product(al, bh))
+
+
 def lanes(shape):
     return lax.broadcasted_iota(jnp.int32, shape, 1)
 
@@ -45,11 +49,11 @@
 
 
 def gram_packed(left, right):
-    return dot_nt(left, stacked_rows(right, turned(right)), HIGH)
+    return in_parts(dot_nt, left, stacked_rows(right, turned(right)))
 
 
 def gram_planes(re, im):
-    return dot_nt(re, stacked_rows(re, im), HIGH) + dot_nt(im, stacked_rows(im, -re), HIGH)
+    return in_parts(dot_nt, re, stacked_rows(re, im)) + in_parts(dot_nt, im, stacked_rows(im, -re))
 
 
 def planes_of(packed):
@@ -59,12 +63,12 @@
 
 def apply_packed(matrix, packed):
     re, im = planes_of(matrix)
-    return dot(re[:, :K], packed, HIGH) - dot(im[:, :K], turned(packed), HIGH)
+    return in_parts(dot, re[:, :K], packed) - in_parts(dot, im[:, :K], turned(packed))
 
 
 def conj_apply_packed(matrix, packed):
     re, im = planes_of(matrix)
-    return dot(re[:, :K], packed, HIGH) + dot(im[:, :K], turned(packed), HIGH)
+    return in_parts(dot, re[:, :K], packed) + in_parts(dot, im[:, :K], turned(packed))
 
 
 def embedded(matrix):
@@ -74,47 +78,57 @@
     return jnp.concatenate([upper, lower], axis=0)[:, : 2 * K]
 
 
-def factor_steps(gram, result):
+def factor_start(gram):
     lane = lanes((K, 128))
     row = lax.broadcasted_iota(jnp.int32, (K, 128), 0)
     low = lane < 64
     re = jnp.where(low, gram, jnp.where(lane - 64 == row, 1.0, 0.0))
     im = jnp.where(low, pltpu.roll(gram, 64, 1), 0.0)
-    done_re, done_im = [], []
-    for base in range(0, K, 8):
-        below = lax.broadcasted_iota(jnp.int32, (K - base, 1), 0)
-        for s in range(8):
-            j = base + s
-            row_re, row_im = re[s : s + 1], im[s : s + 1]
-            inv = 1.0 / re[s : s + 1, j : j + 1]
-            m_re = jnp.where(below > s, re[:, j : j + 1] * inv, 0.0)
-            m_im = jnp.where(below > s, im[:, j : j + 1] * inv, 0.0)
-            re, im = (
-                re - (m_re * row_re - m_im * row_im),
-                im - (m_re * row_im + m_im * row_re),
+    return tuple(plane[t : t + 8] for plane in (re, im) for t in range(0, K, 8))
+
+
+def factor_block(block, tiles):
+    n = K // 8
+    re, im = list(tiles[:n]), list(tiles[n:])
+    below = lax.broadcasted_iota(jnp.int32, (8, 1), 0)
+    open_tile = [None] + [jnp.where(block + t < n, 1.0, 0.0) for t in range(1, n)]
+    for s in range(8):
+        row_re, row_im = re[0][s : s + 1], im[0][s : s + 1]
+        inv = 1.0 / row_re[:, s : s + 1]
+        for t in range(n):
+            if t == 0:
+                m_re = jnp.where(below > s, re[t][:, s : s + 1] * inv, 0.0)
+                m_im = jnp.where(below > s, im[t][:, s : s + 1] * inv, 0.0)
+            else:
+                m_re = re[t][:, s : s + 1] * (inv * open_tile[t])
+                m_im = im[t][:, s : s + 1] * (inv * open_tile[t])
+            re[t], im[t] = (
+                re[t] - (m_re * row_re - m_im * row_im),
+                im[t] - (m_re * row_im + m_im * row_re),
             )
-        done_re.append(re[:8])
-        done_im.append(im[:8])
-        re, im = re[8:], im[8:]
-        yield
-    re = jnp.concatenate(done_re, axis=0)
-    im = jnp.concatenate(done_im, axis=0)
+    moved = [pltpu.roll(tile, 128 - 8, 1) for tile in re[1:] + re[:1] + im[1:] + im[:1]]
+    return tuple(moved)
+
+
+def factor_end(tiles):
+    n = K // 8
+    re = pltpu.roll(jnp.concatenate(tiles[:n], axis=0), K, 1)
+    im = pltpu.roll(jnp.concatenate(tiles[n:], axis=0), K, 1)
+    lane = lanes((K, 128))
+    row = lax.broadcasted_iota(jnp.int32, (K, 128), 0)
     pivot = jnp.sum(jnp.where(lane == row, re, 0.0), axis=1, keepdims=True)
     scale = 1.0 / jnp.sqrt(pivot)
-    result.append(jnp.where(low, pltpu.roll(re, 64, 1), im) * scale)
+    return jnp.where(lane < 64, pltpu.roll(re, 64, 1), im) * scale
 
 
 def inverse_factor(gram):
-    result = []
-    for _ in factor_steps(gram, result):
-        pass
-    return result[0]
+    return factor_end(lax.fori_loop(0, K // 8, factor_block, factor_start(gram)))
 
 
 def both_sides(matrix, packed):
     left = conj_apply_packed(matrix, packed)
     low = lanes(matrix.shape) < 64
-    return dot_nt(left, stacked_rows(jnp.where(low, matrix, -matrix), pltpu.roll(matrix, 64, 1)), HIGH)
+    return in_parts(dot_nt, left, stacked_rows(jnp.where(low, matrix, -matrix), pltpu.roll(matrix, 64, 1)))
 
 
 def pack_pair(re, im):
@@ -124,6 +138,24 @@
     return even, odd
 
 
+def pack_hermitian(first, second):
+    lane, row = lanes(first.shape), lax.broadcasted_iota(jnp.int32, first.shape, 0)
+    one = jnp.where(lane >= row, first, pltpu.roll(first, 64, 1))
+    two = jnp.where(lane - 64 >= row, pltpu.roll(second, 64, 1), second)
+    return jnp.where(lane < 64, one, two)
+
+
+def unpack_hermitian(both):
+    lane, row = lanes((K, 128)), lax.broadcasted_iota(jnp.int32, (K, 128), 0)
+    column = lane & 63
+    flipped = jnp.concatenate([both, jnp.zeros((128 - K, 128), F32)], axis=0).T
+    other = jnp.where(lane < 64, flipped[:K], pltpu.roll(flipped[64 : 64 + K], 64, 1))
+    re = jnp.where(column >= row, both, other)
+    im = jnp.where(column < row, both, jnp.where(column > row, -other, 0.0))
+    low = lane < 64
+    return jnp.where(low, re, pltpu.roll(im, 64, 1)), jnp.where(low, pltpu.roll(re, 64, 1), im)
+
+
 def unpack_pair(even, odd):
     low = lanes(even.shape) < 64
     re = jnp.where(low, even, pltpu.roll(odd, 64, 1))
@@ -141,7 +173,7 @@
 
 def kernel(coupling, initial, basis, ritz, *scratch):
     (
-        stage, hhi, hlo, lhs, part, rsx, mixed, red, rsz, gath, ybuf, acc, acc2,
+        stage, hhi, hlo, lhs, part, rsx, red, rsz, gath, ybuf, acc, acc2,
         pk, rsy, gy, scat, ypc, gsrc, gyc, gxs, gx, gzs, gz,
         g4, g4y, g4x, g4z, psrc, py, px, pz, pall,
         hsem, rsx_s, rsx_r, rsz_s, rsz_r, agz_s, agz_r, agx_s, agx_r,
@@ -182,9 +214,6 @@
     def near(k):
         return (z + 8 - near_first(k)) & 7
 
-    def side(k):
-        return 1 - 2 * (k & 1)
-
     def load(k):
         columns = pl.ds(pl.multiple_of(far(k) * CH, CH), CH)
         return pltpu.make_async_copy(coupling.at[:, :, columns], stage.at[far(k)], hsem.at[far(k)])
@@ -204,11 +233,9 @@
         lhs[...] = jnp.concatenate([high, low], axis=0)
 
 
-    def x_part(k, which):
-        zc, s = far(k), side(k)
-        source = [part.at[zc, rows_of(2)], part.at[zc, rows_of(-s)], mixed.at[zc]][which]
+    def x_part(j, zc):
         return remote(
-            source, rsx.at[which, zc], rsx_s.at[which, zc], rsx_r.at[which, zc], at_x([s, -s, s][which])
+            part.at[zc, rows_of(j)], rsx.at[j - 1, zc], rsx_s.at[j - 1, zc], rsx_r.at[j - 1, zc], at_x(j)
         )
 
     def z_part(k):
@@ -216,8 +243,8 @@
         return remote(red.at[far(k)], rsz.at[o], rsz_s.at[o], rsz_r.at[o], at_z(o))
 
     def send_parts(k):
-        x_part(k, 0).start()
-        x_part(k, 1).start()
+        for j in range(1, X):
+            x_part(j, far(k)).start()
 
     def column_product(load_first, send):
         def chunk(k):
@@ -235,20 +262,14 @@
 
         loop(Z, chunk)
 
-    def column_mix():
-        def chunk(k):
-            x_part(k, 0).wait_recv()
-            mixed[far(k)] = part[far(k), rows_of(side(k))] + rsx[0, far(k)]
-            x_part(k, 2).start()
-
-        loop(Z, chunk)
-
     def column_sum():
         def chunk(k):
             zc = far(k)
-            x_part(k, 1).wait_recv()
-            x_part(k, 2).wait_recv()
-            red[zc] = part[zc, rows_of(0)] + rsx[1, zc] + rsx[2, zc]
+            total = part[zc, rows_of(0)]
+            for j in range(1, X):
+                x_part(j, zc).wait_recv()
+                total = total + rsx[j - 1, zc]
+            red[zc] = total
 
             @pl.when(k < Z - 1)
             def _():
@@ -261,48 +282,49 @@
         block = gath.at[zc, rows_of(0)]
         return remote(block, block, agz_s.at[o], agz_r.at[o], at_z(o))
 
-    def x_whole(k, which, sent=True):
-        zc, s = near(k), side(k)
-        straight = k >= Z - 2
-        shift = 0 if sent and (which < 2 or straight) else (-s if sent else [-s, s, 2][which])
+    def x_whole(j, zc, shift):
         block = gath.at[zc, rows_of(shift)]
-        dev = at_x([s, -s, 2 if straight else s][which])
-        return remote(block, block, agx_s.at[which, k], agx_r.at[which, k], dev)
-
-    def column_gather(steps):
-        total = red[z]
-        for k in range(Z - 1):
+        return remote(block, block, agx_s.at[j - 1, zc], agx_r.at[j - 1, zc], at_x(j))
+
+    def column_gather(tiles):
+        def last(k, total):
             z_part(k).wait_recv()
-            total = total + rsz[far_first(k)]
-        gath[z, rows_of(0)] = total
-        for k in range(Z - 1):
-            z_whole(far_first(k), z).start()
-
-        def pass_on(k):
-            x_whole(k, 0, False).wait_recv()
-            x_whole(k, 2).start()
-
-        for k in range(Z):
-            if k > 0:
-                z_whole(near_first(k), near(k)).wait_recv()
-            x_whole(k, 0).start()
-            x_whole(k, 1).start()
-            if k >= Z - 2:
-                x_whole(k, 2).start()
-            if k >= 2:
-                pass_on(k - 2)
-            next(steps, None)
-        for _ in steps:
-            pass
+            return total + rsz[far_first(k)]
+
+        gath[z, rows_of(0)] = lax.fori_loop(0, Z - 1, last, red[z])
+        loop(Z - 1, lambda k: z_whole(far_first(k), z).start())
+        for j in range(1, X):
+            x_whole(j, z, 0).start()
+
+        def forward(k):
+            z_whole(near_first(k), near(k)).wait_recv()
+            for j in range(1, X):
+                x_whole(j, near(k), 0).start()
+
+        def step(k, tiles):
+            tiles = factor_block(k, tiles)
+            forward(k + 1)
+            return tiles
+
+        if tiles is None:
+            loop(Z - 1, lambda k: forward(k + 1))
+            return None
+        tiles = lax.fori_loop(0, K // 8, step, tiles)
+        forward(Z - 1)
+        return factor_end(tiles)
 
     def column_sent():
-        for k in range(Z):
-            for which in range(3):
-                x_part(k, which).wait_send()
-                x_whole(k, which).wait_send()
-            if k < Z - 1:
+        def chunk(k):
+            for j in range(1, X):
+                x_part(j, k).wait_send()
+                x_whole(j, k, 0).wait_send()
+
+            @pl.when(k < Z - 1)
+            def _():
                 z_part(k).wait_send()
                 z_whole(far_first(k), z).wait_send()
+
+        loop(Z, chunk)
 
     def c_gram(t, k):
         return remote(gsrc, gyc.at[t, k], gyc_s.at[t, k], gyc_r.at[t, k], at_c(k))
@@ -317,22 +339,21 @@
         acc[...] = jnp.zeros_like(acc)
         acc2[...] = jnp.zeros_like(acc2)
         gsrc[...] = jnp.zeros_like(gsrc)
-        for k in range(Z):
+
+        def receive(k):
             zc = near(k)
-            if k < Z - 2:
-                x_whole(k, 1, False).wait_recv()
-                x_whole(k, 2, False).wait_recv()
-            else:
-                for which in range(3):
-                    x_whole(k, which, False).wait_recv()
+            for j in range(1, X):
+                x_whole(j, zc, X - j).wait_recv()
             block = gath[zc]
             if factor is not None:
-                block = dot(factor, block, HIGH)
+                block = in_parts(dot, factor, block)
             ybuf[zc] = block
             high, low = split(block)
             acc[...] += dot_nt(jnp.concatenate([high, low], axis=0), hhi[zc])
             acc2[...] += dot_nt(high, hlo[zc])
             gsrc[...] += gram_planes(block[:K], block[K:])
+
+        loop(Z, receive)
         for k in range(1, C):
             c_gram(t, k).start()
         total = acc[: 2 * K] + acc[2 * K :] + acc2[...]
@@ -388,16 +409,14 @@
 
     v_re, v_im = initial[0], initial[1]
     set_left(v_re, v_im)
-    column_product(True, False)
     pl.semaphore_wait(barrier, len(partners))
-    loop(Z, send_parts)
+    column_product(True, True)
     for q in range(4):
         even, odd = pack_pair(v_re[:, 128 * q : 128 * q + 128], v_im[:, 128 * q : 128 * q + 128])
         pk[2 * q], pk[2 * q + 1] = even, odd
     v_piece = pk[c]
-    column_mix()
     column_sum()
-    column_gather(iter(()))
+    column_gather(None)
     row_product(0, None)
     z2_piece = row_sum()
     gy[c] = z2_piece
@@ -415,9 +434,8 @@
     block = jnp.concatenate(
         [jnp.concatenate([pair[p] for pair in pairs], axis=1) for p in range(2)], axis=0
     )
-    block = dot(embedded(inv1), block, HIGH)
+    block = in_parts(dot, embedded(inv1), block)
     set_left(block[:K], block[K:])
-    column_product(False, True)
     gxs[...] = gram_planes(block[:K], block[K:])
 
     def x_gram(j):
@@ -428,12 +446,7 @@
 
     for j in range(1, X):
         x_gram(j).start()
-    column_mix()
-    row_sent(0)
-    y2_piece = apply_packed(inv1, z2_piece)
-    y1_piece = scattered(0)
-    psrc[:K] = gram_packed(v_piece, y1_piece)
-    psrc[K : 2 * K] = conj_apply_packed(inv1, gram_packed(y1_piece, y2_piece))
+    column_product(False, True)
     total = gxs[...]
     for j in range(1, X):
         x_gram(j).wait_recv()
@@ -441,14 +454,17 @@
     gzs[...] = total
     for o in range(1, Z):
         z_gram(o).start()
+    row_sent(0)
+    y2_piece = apply_packed(inv1, z2_piece)
+    y1_piece = scattered(0)
+    psrc[:K] = gram_packed(v_piece, y1_piece)
+    psrc[K : 2 * K] = conj_apply_packed(inv1, gram_packed(y1_piece, y2_piece))
     column_sum()
     total = gzs[...]
     for o in range(1, Z):
         z_gram(o).wait_recv()
         total = total + gz[o]
-    inv2 = []
-    column_gather(factor_steps(total * (1.0 / N), inv2))
-    inv2 = inv2[0]
+    inv2 = column_gather(factor_start(total * (1.0 / N)))
     row_product(1, embedded(inv2))
     z4_piece = row_sum()
 
@@ -483,48 +499,43 @@
             total = total + slots[i]
         return total
 
-    gram = gram_packed(z4_piece, z4_piece)
-    g4[0] = gram
+    y3_piece = scattered(1)
+    both = pack_hermitian(gram_packed(z4_piece, z4_piece), gram_packed(y3_piece, z4_piece))
+    g4[0] = both
     for k in range(1, C):
         g_c(k).start()
+    psrc[2 * K : 3 * K] = conj_apply_packed(inv2, gram_packed(y2_piece, y3_piece))
+    psrc[3 * K :] = jnp.zeros((K, 128), F32)
+    for k in range(1, C):
+        p_c(k).start()
     inv3 = c_factor(1)
-    gram = both_sides(inv3, added(gram, C, g_c, g4y))
-    g4[1] = gram
+    y4_piece = apply_packed(inv3, z4_piece)
+    both = added(both, C, g_c, g4y)
+    g4[1] = both
     for j in range(1, X):
         g_x(j).start()
-    y4_piece = apply_packed(inv3, z4_piece)
-    y3_piece = scattered(1)
-    psrc[2 * K : 3 * K] = conj_apply_packed(inv2, gram_packed(y2_piece, y3_piece))
-    psrc[3 * K :] = conj_apply_packed(inv3, gram_packed(y3_piece, y4_piece))
-    for k in range(1, C):
-        p_c(k).start()
-    gram = added(gram, X, g_x, g4x)
-    g4[2] = gram
-    for o in range(1, Z):
-        g_z(o).start()
     px[0] = added(psrc[slab(0)], C, p_c, py)
     for j in range(1, X):
         p_x(j).start()
+    both = added(both, X, g_x, g4x)
+    g4[2] = both
+    for o in range(1, Z):
+        g_z(o).start()
     pz[0] = added(px[0], X, p_x, px)
     for o in range(1, Z):
         p_z(o).start()
-    gram = added(gram, Z, g_z, g4z)
-    value = []
-    steps = factor_steps(gram * (1.0 / N), value)
-    for _ in range(3):
-        next(steps)
+    both = added(both, Z, g_z, g4z) * (1.0 / N)
     pall[slab(0)] = added(pz[0], Z, p_z, pz) * (1.0 / N)
     for k in range(1, C):
         p_all(k, 0).start()
-    for _ in steps:
-        pass
-    value = apply_packed(value[0], y4_piece)
+    gram, projection = unpack_hermitian(both)
+    value = apply_packed(inverse_factor(both_sides(inv3, gram)), y4_piece)
     basis[0] = value[:, :64]
     basis[1] = pltpu.roll(value, 64, 1)[:, :64]
     for k in range(1, C):
         p_all(k, C - k).wait_recv()
     for t in range(ITERS):
-        value = pall[K * t : K * t + K]
+        value = pall[K * t : K * t + K] if t < ITERS - 1 else both_sides(inv3, projection)
         ritz[t, 0] = value[:, :K]
         ritz[t, 1] = pltpu.roll(value, 64, 1)[:, :K]
 
@@ -555,7 +566,6 @@
         pltpu.VMEM((4 * K, 1024), BF16),
         pltpu.VMEM((Z, 2 * K, CH), F32),
         pltpu.VMEM((3, Z, RB, CH), F32),
-        pltpu.VMEM((Z, RB, CH), F32),
         pltpu.VMEM((Z, RB, CH), F32),
         pltpu.VMEM((Z, RB, CH), F32),
         pltpu.VMEM((Z, 2 * K, CH), F32),

time: 132 us -> 116 us (0.88)
  Pallas kernels: 128 us -> 112 us
    pallas_call x1, Pallas kernels: 128 us -> 112 us  [body(): pl.pallas_call(kernel, name='subspace', out_shape=(jax.ShapeDtypeStruct((...]
where the time goes in v4:
time: 116 us
  Pallas kernels  112 us (97%)
  local copies, waits for them, and re-layouts  3.04 us (3%)
    pallas_call x1, Pallas kernels, body(): pl.pallas_call(kernel, name='subspace', out_shape=(jax.ShapeDtypeStruct((...  112 us
    unnamed x2, local copies, waits for them, and re-layouts  3.04 us

profile of v4, /device:TPU:1, one launch (start us, length us, event | category | flops | bytes accessed | tf_op | source)
XLA Modules:
  0.0 115.8 jit_solution(18407872795988496636)
XLA Ops:
  0.6 112.2 %subspace.1 = (f32[2,48,64]{2,1,0:T(8,128)}, f32[4,2,48,48]{3,2,1,0:T(8,128)}) custom-call(f32[2,512,2048]{2,1,0:T(8,128)} %coupling.1, f32[2,48,512]{2,1,0:T(8,128)} %initial.1), custom_call_target="tpu_custom_call" | custom-call | tf_op jit(solution)/shard_map/subspace/pallas_call | solution.py:607
  112.8 1.4 %copy.6 = f32[2,48,64]{2,1,0:T(8,128)} copy(f32[2,48,64]{2,1,0:T(8,128)} %get-tuple-element.4) | data formatting | bytes 49152
  114.2 1.6 %copy.7 = f32[4,2,48,48]{3,2,1,0:T(8,128)} copy(f32[4,2,48,48]{3,2,1,0:T(8,128)} %get-tuple-element.5) | data formatting | bytes 147456

commit v5 on v4

--- a/solution.py
+++ b/solution.py
@@ -138,22 +138,22 @@
     return even, odd
 
 
-def pack_hermitian(first, second):
-    lane, row = lanes(first.shape), lax.broadcasted_iota(jnp.int32, first.shape, 0)
-    one = jnp.where(lane >= row, first, pltpu.roll(first, 64, 1))
-    two = jnp.where(lane - 64 >= row, pltpu.roll(second, 64, 1), second)
-    return jnp.where(lane < 64, one, two)
-
-
-def unpack_hermitian(both):
+def pack_triangle(packed):
+    lane, row = lanes(packed.shape), lax.broadcasted_iota(jnp.int32, packed.shape, 0)
+    one = jnp.where(lane >= row, packed, pltpu.roll(packed, 64, 1))
+    return jnp.where(lane[:RB] < 64, one[:RB], pltpu.roll(one[RB:], 64, 1))
+
+
+def unpack_triangle(half):
+    low = lanes(half.shape) < 64
+    upper = jnp.where(low, half, 0.0)
+    lower = jnp.where(low, pltpu.roll(half, 64, 1), 0.0)
+    tri = jnp.concatenate([upper, lower], axis=0)
     lane, row = lanes((K, 128)), lax.broadcasted_iota(jnp.int32, (K, 128), 0)
-    column = lane & 63
-    flipped = jnp.concatenate([both, jnp.zeros((128 - K, 128), F32)], axis=0).T
-    other = jnp.where(lane < 64, flipped[:K], pltpu.roll(flipped[64 : 64 + K], 64, 1))
-    re = jnp.where(column >= row, both, other)
-    im = jnp.where(column < row, both, jnp.where(column > row, -other, 0.0))
-    low = lane < 64
-    return jnp.where(low, re, pltpu.roll(im, 64, 1)), jnp.where(low, pltpu.roll(re, 64, 1), im)
+    other = jnp.concatenate([tri, jnp.zeros((128 - K, 128), F32)], axis=0).T[:K]
+    re = jnp.where(lane >= row, tri, other)
+    im = jnp.where(lane < row, tri, jnp.where(lane > row, -other, 0.0))
+    return jnp.where(lane < 64, re, pltpu.roll(im, 64, 1))
 
 
 def unpack_pair(even, odd):
@@ -174,7 +174,7 @@
 def kernel(coupling, initial, basis, ritz, *scratch):
     (
         stage, hhi, hlo, lhs, part, rsx, red, rsz, gath, ybuf, acc, acc2,
-        pk, rsy, gy, scat, ypc, gsrc, gyc, gxs, gx, gzs, gz,
+        pk, rsy, gy, scat, ypc, gsum, gsrc, gyc, gxs, gx, gzs, gz,
         g4, g4y, g4x, g4z, psrc, py, px, pz, pall,
         hsem, rsx_s, rsx_r, rsz_s, rsz_r, agz_s, agz_r, agx_s, agx_r,
         rsy_s, rsy_r, agy_s, agy_r, sc_s, sc_r, gyc_s, gyc_r, gx_s, gx_r, gz_s, gz_r,
@@ -338,7 +338,7 @@
     def row_product(t, factor):
         acc[...] = jnp.zeros_like(acc)
         acc2[...] = jnp.zeros_like(acc2)
-        gsrc[...] = jnp.zeros_like(gsrc)
+        gsum[...] = jnp.zeros_like(gsum)
 
         def receive(k):
             zc = near(k)
@@ -351,11 +351,9 @@
             high, low = split(block)
             acc[...] += dot_nt(jnp.concatenate([high, low], axis=0), hhi[zc])
             acc2[...] += dot_nt(high, hlo[zc])
-            gsrc[...] += gram_planes(block[:K], block[K:])
+            gsum[...] += gram_planes(block[:K], block[K:])
 
         loop(Z, receive)
-        for k in range(1, C):
-            c_gram(t, k).start()
         total = acc[: 2 * K] + acc[2 * K :] + acc2[...]
         re = total[:K, :512] - total[K:, 512:]
         im = total[K:, :512] + total[:K, 512:]
@@ -376,6 +374,10 @@
                 c_scatter(t, k).start()
             ypc[t] = scat[t, c]
 
+        gsrc[...] = pack_triangle(gsum[...])
+        for k in range(1, C):
+            c_gram(t, k).start()
+
     def row_sum():
         total = pk[c]
         for k in range(1, C):
@@ -388,7 +390,7 @@
         for k in range(1, C):
             c_gram(t, k).wait_recv()
             total = total + gyc[t, k]
-        return inverse_factor(total * (1.0 / N))
+        return inverse_factor(unpack_triangle(total * (1.0 / N)))
 
     def scattered(t):
         @pl.when(c != z)
@@ -436,7 +438,7 @@
     )
     block = in_parts(dot, embedded(inv1), block)
     set_left(block[:K], block[K:])
-    gxs[...] = gram_planes(block[:K], block[K:])
+    gxs[...] = pack_triangle(gram_planes(block[:K], block[K:]))
 
     def x_gram(j):
         return remote(gxs, gx.at[j], gx_s.at[j], gx_r.at[j], at_x(j))
@@ -464,19 +466,19 @@
     for o in range(1, Z):
         z_gram(o).wait_recv()
         total = total + gz[o]
-    inv2 = column_gather(factor_start(total * (1.0 / N)))
+    inv2 = column_gather(factor_start(unpack_triangle(total * (1.0 / N))))
     row_product(1, embedded(inv2))
     z4_piece = row_sum()
 
 
-    def g_c(k):
-        return remote(g4.at[0], g4y.at[k], g4y_s.at[k], g4y_r.at[k], at_c(k))
-
-    def g_x(j):
-        return remote(g4.at[1], g4x.at[j], g4x_s.at[j], g4x_r.at[j], at_x(j))
-
-    def g_z(o):
-        return remote(g4.at[2], g4z.at[o], g4z_s.at[o], g4z_r.at[o], at_z(o))
+    def g_c(m, k):
+        return remote(g4.at[m, 0], g4y.at[m, k], g4y_s.at[m, k], g4y_r.at[m, k], at_c(k))
+
+    def g_x(m, j):
+        return remote(g4.at[m, 1], g4x.at[m, j], g4x_s.at[m, j], g4x_r.at[m, j], at_x(j))
+
+    def g_z(m, o):
+        return remote(g4.at[m, 2], g4z.at[m, o], g4z_s.at[m, o], g4z_r.at[m, o], at_z(o))
 
     def slab(shift):
         return pl.ds(pl.multiple_of(((c + shift) & 7) * RB, 8), RB)
@@ -499,60 +501,88 @@
             total = total + slots[i]
         return total
 
+    def last_start(m, total):
+        g4[m, 0] = total
+        for k in range(1, C):
+            g_c(m, k).start()
+        return total
+
+    def last_x(m, total):
+        for k in range(1, C):
+            g_c(m, k).wait_recv()
+            total = total + g4y[m, k]
+        g4[m, 1] = total
+        for j in range(1, X):
+            g_x(m, j).start()
+        return total
+
+    def last_z(m, total):
+        for j in range(1, X):
+            g_x(m, j).wait_recv()
+            total = total + g4x[m, j]
+        g4[m, 2] = total
+        for o in range(1, Z):
+            g_z(m, o).start()
+        return total
+
+    def last_end(m, total):
+        for o in range(1, Z):
+            g_z(m, o).wait_recv()
+            total = total + g4z[m, o]
+        return unpack_triangle(total * (1.0 / N))
+
+    gram = last_start(0, pack_triangle(gram_packed(z4_piece, z4_piece)))
     y3_piece = scattered(1)
-    both = pack_hermitian(gram_packed(z4_piece, z4_piece), gram_packed(y3_piece, z4_piece))
-    g4[0] = both
-    for k in range(1, C):
-        g_c(k).start()
+    projection = last_start(1, pack_triangle(gram_packed(y3_piece, z4_piece)))
     psrc[2 * K : 3 * K] = conj_apply_packed(inv2, gram_packed(y2_piece, y3_piece))
     psrc[3 * K :] = jnp.zeros((K, 128), F32)
     for k in range(1, C):
         p_c(k).start()
     inv3 = c_factor(1)
+    gram = last_x(0, gram)
     y4_piece = apply_packed(inv3, z4_piece)
-    both = added(both, C, g_c, g4y)
-    g4[1] = both
-    for j in range(1, X):
-        g_x(j).start()
+    projection = last_x(1, projection)
+    gram = last_z(0, gram)
     px[0] = added(psrc[slab(0)], C, p_c, py)
     for j in range(1, X):
         p_x(j).start()
-    both = added(both, X, g_x, g4x)
-    g4[2] = both
-    for o in range(1, Z):
-        g_z(o).start()
+    projection = last_z(1, projection)
     pz[0] = added(px[0], X, p_x, px)
     for o in range(1, Z):
         p_z(o).start()
-    both = added(both, Z, g_z, g4z) * (1.0 / N)
+    column_sent()
+    row_sent(1)
+    for k in range(1, C):
+        c_whole(k, c).wait_send()
+        for m in range(2):
+            g_c(m, k).wait_send()
+        p_c(k).wait_send()
+    for j in range(1, X):
+        x_gram(j).wait_send()
+        for m in range(2):
+            g_x(m, j).wait_send()
+        p_x(j).wait_send()
+    for o in range(1, Z):
+        z_gram(o).wait_send()
+    gram = both_sides(inv3, last_end(0, gram))
     pall[slab(0)] = added(pz[0], Z, p_z, pz) * (1.0 / N)
     for k in range(1, C):
         p_all(k, 0).start()
-    gram, projection = unpack_hermitian(both)
-    value = apply_packed(inverse_factor(both_sides(inv3, gram)), y4_piece)
+    value = apply_packed(inverse_factor(gram), y4_piece)
     basis[0] = value[:, :64]
     basis[1] = pltpu.roll(value, 64, 1)[:, :64]
     for k in range(1, C):
         p_all(k, C - k).wait_recv()
     for t in range(ITERS):
-        value = pall[K * t : K * t + K] if t < ITERS - 1 else both_sides(inv3, projection)
+        value = pall[K * t : K * t + K] if t < ITERS - 1 else both_sides(inv3, last_end(1, projection))
         ritz[t, 0] = value[:, :K]
         ritz[t, 1] = pltpu.roll(value, 64, 1)[:, :K]
 
-    column_sent()
-    row_sent(1)
     for k in range(1, C):
-        c_whole(k, c).wait_send()
-        g_c(k).wait_send()
-        p_c(k).wait_send()
         p_all(k, 0).wait_send()
-    for j in range(1, X):
-        x_gram(j).wait_send()
-        g_x(j).wait_send()
-        p_x(j).wait_send()
     for o in range(1, Z):
-        z_gram(o).wait_send()
-        g_z(o).wait_send()
+        for m in range(2):
+            g_z(m, o).wait_send()
         p_z(o).wait_send()
 
 
@@ -578,15 +608,16 @@
         pltpu.VMEM((2, C, *packed), F32),
         pltpu.VMEM((2, *packed), F32),
         pltpu.VMEM(packed, F32),
-        pltpu.VMEM((2, C, *packed), F32),
-        pltpu.VMEM(packed, F32),
-        pltpu.VMEM((X, *packed), F32),
-        pltpu.VMEM(packed, F32),
-        pltpu.VMEM((Z, *packed), F32),
-        pltpu.VMEM((3, *packed), F32),
-        pltpu.VMEM((C, *packed), F32),
-        pltpu.VMEM((X, *packed), F32),
-        pltpu.VMEM((Z, *packed), F32),
+        pltpu.VMEM(piece, F32),
+        pltpu.VMEM((2, C, *piece), F32),
+        pltpu.VMEM(piece, F32),
+        pltpu.VMEM((X, *piece), F32),
+        pltpu.VMEM(piece, F32),
+        pltpu.VMEM((Z, *piece), F32),
+        pltpu.VMEM((2, 3, *piece), F32),
+        pltpu.VMEM((2, C, *piece), F32),
+        pltpu.VMEM((2, X, *piece), F32),
+        pltpu.VMEM((2, Z, *piece), F32),
         pltpu.VMEM((4 * K, 128), F32),
         pltpu.VMEM((C, *piece), F32),
         pltpu.VMEM((X, *piece), F32),
@@ -598,7 +629,7 @@
         dma((C,)), dma((C,)), dma((C,)), dma((C,)),
         dma((2, C)), dma((2,)), dma((2, C)), dma((2, C)),
         dma((X,)), dma((X,)), dma((Z,)), dma((Z,)),
-        dma((C,)), dma((C,)), dma((X,)), dma((X,)), dma((Z,)), dma((Z,)),
+        dma((2, C)), dma((2, C)), dma((2, X)), dma((2, X)), dma((2, Z)), dma((2, Z)),
         dma((C,)), dma((C,)), dma((X,)), dma((X,)), dma((Z,)), dma((Z,)), dma((C,)), dma((C,)),
     ]
     vmem = pl.BlockSpec(memory_space=pltpu.VMEM)

time: 116 us -> 114 us (0.983)
  Pallas kernels: 112 us -> 110 us
    pallas_call x1, Pallas kernels: 112 us -> 110 us  [body(): pl.pallas_call(kernel, name='subspace', out_shape=(jax.ShapeDtypeStruct((...]
where the time goes in v5:
time: 114 us
  Pallas kernels  110 us (96%)
  local copies, waits for them, and re-layouts  3.04 us (3%)
    pallas_call x1, Pallas kernels, body(): pl.pallas_call(kernel, name='subspace', out_shape=(jax.ShapeDtypeStruct((...  110 us
    unnamed x2, local copies, waits for them, and re-layouts  3.04 us

profile of v5, /device:TPU:1, one launch (start us, length us, event | category | flops | bytes accessed | tf_op | source)
XLA Modules:
  0.0 113.7 jit_solution(9911077520047322632)
XLA Ops:
  0.6 110.0 %subspace.1 = (f32[2,48,64]{2,1,0:T(8,128)}, f32[4,2,48,48]{3,2,1,0:T(8,128)}) custom-call(f32[2,512,2048]{2,1,0:T(8,128)} %coupling.1, f32[2,48,512]{2,1,0:T(8,128)} %initial.1), custom_call_target="tpu_custom_call" | custom-call | tf_op jit(solution)/shard_map/subspace/pallas_call | solution.py:638
  110.7 1.4 %copy.6 = f32[2,48,64]{2,1,0:T(8,128)} copy(f32[2,48,64]{2,1,0:T(8,128)} %get-tuple-element.4) | data formatting | bytes 49152
  112.1 1.6 %copy.7 = f32[4,2,48,48]{3,2,1,0:T(8,128)} copy(f32[4,2,48,48]{3,2,1,0:T(8,128)} %get-tuple-element.5) | data formatting | bytes 147456

commit v6 on v5

--- a/solution.py
+++ b/solution.py
@@ -176,7 +176,7 @@
         stage, hhi, hlo, lhs, part, rsx, red, rsz, gath, ybuf, acc, acc2,
         pk, rsy, gy, scat, ypc, gsum, gsrc, gyc, gxs, gx, gzs, gz,
         g4, g4y, g4x, g4z, psrc, py, px, pz, pall,
-        hsem, rsx_s, rsx_r, rsz_s, rsz_r, agz_s, agz_r, agx_s, agx_r,
+        hsem, big, rw_s, rw_r, aw_s, aw_r, rsx_s, rsx_r, rsz_s, rsz_r, agz_s, agz_r, agx_s, agx_r,
         rsy_s, rsy_r, agy_s, agy_r, sc_s, sc_r, gyc_s, gyc_r, gx_s, gx_r, gz_s, gz_r,
         g4y_s, g4y_r, g4x_s, g4x_r, g4z_s, g4z_r, py_s, py_r, px_s, px_r, pz_s, pz_r, pa_s, pa_r,
     ) = scratch
@@ -243,8 +243,11 @@
         return remote(red.at[far(k)], rsz.at[o], rsz_s.at[o], rsz_r.at[o], at_z(o))
 
     def send_parts(k):
-        for j in range(1, X):
+        for j in (1, 3, 2):
             x_part(j, far(k)).start()
+
+    def whole_part():
+        return remote(part.at[far(0)], big, rw_s.at[0], rw_r.at[0], at_z(4))
 
     def column_product(load_first, send):
         def chunk(k):
@@ -258,13 +261,28 @@
             both = dot(lhs[...], hhi[zc])
             part[zc] = both[: 2 * K] + both[2 * K :] + dot(lhs[: 2 * K], hlo[zc])
             if send:
-                send_parts(k)
+
+                @pl.when(k == 0)
+                def _():
+                    whole_part().start()
+
+                @pl.when((k > 0) & (k < Z - 1))
+                def _():
+                    send_parts(k)
 
         loop(Z, chunk)
 
     def column_sum():
-        def chunk(k):
+        def chunk(i):
+            k = i + 1
             zc = far(k)
+
+            @pl.when(k == 5)
+            def _():
+                whole_part().wait_recv()
+                part[z] = part[z] + big[...]
+                send_parts(Z - 1)
+
             total = part[zc, rows_of(0)]
             for j in range(1, X):
                 x_part(j, zc).wait_recv()
@@ -275,7 +293,7 @@
             def _():
                 z_part(k).start()
 
-        loop(Z, chunk)
+        loop(Z - 1, chunk)
 
 
     def z_whole(o, zc):
@@ -285,21 +303,30 @@
     def x_whole(j, zc, shift):
         block = gath.at[zc, rows_of(shift)]
         return remote(block, block, agx_s.at[j - 1, zc], agx_r.at[j - 1, zc], at_x(j))
+
+    def whole_block(zc):
+        return remote(gath.at[zc], gath.at[zc], aw_s.at[0], aw_r.at[0], at_z(4))
 
     def column_gather(tiles):
         def last(k, total):
             z_part(k).wait_recv()
             return total + rsz[far_first(k)]
 
-        gath[z, rows_of(0)] = lax.fori_loop(0, Z - 1, last, red[z])
-        loop(Z - 1, lambda k: z_whole(far_first(k), z).start())
-        for j in range(1, X):
+        gath[z, rows_of(0)] = lax.fori_loop(1, Z - 1, last, red[z])
+        loop(Z - 2, lambda k: z_whole(far_first(k + 1), z).start())
+        for j in (1, 3, 2):
             x_whole(j, z, 0).start()
 
         def forward(k):
             z_whole(near_first(k), near(k)).wait_recv()
-            for j in range(1, X):
+            for j in (1, 3, 2):
                 x_whole(j, near(k), 0).start()
+
+            @pl.when(k == 2)
+            def _():
+                for j in range(1, X):
+                    x_whole(j, z, X - j).wait_recv()
+                whole_block(z).start()
 
         def step(k, tiles):
             tiles = factor_block(k, tiles)
@@ -307,24 +334,26 @@
             return tiles
 
         if tiles is None:
-            loop(Z - 1, lambda k: forward(k + 1))
+            loop(Z - 2, lambda k: forward(k + 1))
             return None
         tiles = lax.fori_loop(0, K // 8, step, tiles)
-        forward(Z - 1)
         return factor_end(tiles)
 
     def column_sent():
-        def chunk(k):
+        def chunk(i):
+            k = i + 1
             for j in range(1, X):
-                x_part(j, k).wait_send()
-                x_whole(j, k, 0).wait_send()
+                x_part(j, far(k)).wait_send()
+                x_whole(j, far(k), 0).wait_send()
 
             @pl.when(k < Z - 1)
             def _():
                 z_part(k).wait_send()
                 z_whole(far_first(k), z).wait_send()
 
-        loop(Z, chunk)
+        loop(Z - 1, chunk)
+        whole_part().wait_send()
+        whole_block(z).wait_send()
 
     def c_gram(t, k):
         return remote(gsrc, gyc.at[t, k], gyc_s.at[t, k], gyc_r.at[t, k], at_c(k))
@@ -342,8 +371,16 @@
 
         def receive(k):
             zc = near(k)
-            for j in range(1, X):
-                x_whole(j, zc, X - j).wait_recv()
+
+            @pl.when((k > 0) & (k < Z - 1))
+            def _():
+                for j in range(1, X):
+                    x_whole(j, zc, X - j).wait_recv()
+
+            @pl.when(k == Z - 1)
+            def _():
+                whole_block(zc).wait_recv()
+
             block = gath[zc]
             if factor is not None:
                 block = in_parts(dot, factor, block)
@@ -624,6 +661,8 @@
         pltpu.VMEM((Z, *piece), F32),
         pltpu.VMEM((4 * K, 128), F32),
         dma((Z,)),
+        pltpu.VMEM((2 * K, CH), F32),
+        dma((1,)), dma((1,)), dma((1,)), dma((1,)),
         dma((3, Z)), dma((3, Z)), dma((Z,)), dma((Z,)),
         dma((Z,)), dma((Z,)), dma((3, Z)), dma((3, Z)),
         dma((C,)), dma((C,)), dma((C,)), dma((C,)),

time: 114 us -> 113 us (level)
  no operation moved by 1% of the time
where the time goes in v6:
time: 113 us
  Pallas kernels  109 us (96%)
  local copies, waits for them, and re-layouts  3.04 us (3%)
    pallas_call x1, Pallas kernels, body(): pl.pallas_call(kernel, name='subspace', out_shape=(jax.ShapeDtypeStruct((...  109 us
    unnamed x2, local copies, waits for them, and re-layouts  3.04 us

profile of v6, /device:TPU:1, one launch (start us, length us, event | category | flops | bytes accessed | tf_op | source)
XLA Modules:
  0.0 112.8 jit_solution(403125793536018258)
XLA Ops:
  0.6 109.1 %subspace.1 = (f32[2,48,64]{2,1,0:T(8,128)}, f32[4,2,48,48]{3,2,1,0:T(8,128)}) custom-call(f32[2,512,2048]{2,1,0:T(8,128)} %coupling.1, f32[2,48,512]{2,1,0:T(8,128)} %initial.1), custom_call_target="tpu_custom_call" | custom-call | tf_op jit(solution)/shard_map/subspace/pallas_call | solution.py:677
  109.8 1.4 %copy.6 = f32[2,48,64]{2,1,0:T(8,128)} copy(f32[2,48,64]{2,1,0:T(8,128)} %get-tuple-element.4) | data formatting | bytes 49152
  111.2 1.6 %copy.7 = f32[4,2,48,48]{3,2,1,0:T(8,128)} copy(f32[4,2,48,48]{3,2,1,0:T(8,128)} %get-tuple-element.5) | data formatting | bytes 147456

commit v7 on v6

--- a/solution.py
+++ b/solution.py
@@ -171,7 +171,16 @@
     return far_first(7 - k) & 7
 
 
-def kernel(coupling, initial, basis, ritz, *scratch):
+def results_kernel(value, projections, basis, ritz):
+    basis[0] = value[:, :64]
+    basis[1] = pltpu.roll(value[...], 64, 1)[:, :64]
+    for t in range(ITERS):
+        packed = projections[K * t : K * t + K]
+        ritz[t, 0] = packed[:, :K]
+        ritz[t, 1] = pltpu.roll(packed, 64, 1)[:, :K]
+
+
+def kernel(coupling, initial, last_value, last_projections, *scratch):
     (
         stage, hhi, hlo, lhs, part, rsx, red, rsz, gath, ybuf, acc, acc2,
         pk, rsy, gy, scat, ypc, gsum, gsrc, gyc, gxs, gx, gzs, gz,
@@ -605,15 +614,11 @@
     pall[slab(0)] = added(pz[0], Z, p_z, pz) * (1.0 / N)
     for k in range(1, C):
         p_all(k, 0).start()
-    value = apply_packed(inverse_factor(gram), y4_piece)
-    basis[0] = value[:, :64]
-    basis[1] = pltpu.roll(value, 64, 1)[:, :64]
+    last_value[...] = apply_packed(inverse_factor(gram), y4_piece)
+    last_projections[3 * K :] = both_sides(inv3, last_end(1, projection))
     for k in range(1, C):
         p_all(k, C - k).wait_recv()
-    for t in range(ITERS):
-        value = pall[K * t : K * t + K] if t < ITERS - 1 else both_sides(inv3, last_end(1, projection))
-        ritz[t, 0] = value[:, :K]
-        ritz[t, 1] = pltpu.roll(value, 64, 1)[:, :K]
+    last_projections[: 3 * K] = pall[: 3 * K]
 
     for k in range(1, C):
         p_all(k, 0).wait_send()
@@ -674,12 +679,12 @@
     vmem = pl.BlockSpec(memory_space=pltpu.VMEM)
 
     def body(coupling, initial):
-        return pl.pallas_call(
+        value, projections = pl.pallas_call(
             kernel,
             name="subspace",
             out_shape=(
-                jax.ShapeDtypeStruct((2, K, 64), F32),
-                jax.ShapeDtypeStruct((ITERS, 2, K, K), F32),
+                jax.ShapeDtypeStruct((K, 128), F32),
+                jax.ShapeDtypeStruct((ITERS * K, 128), F32),
             ),
             in_specs=[pl.BlockSpec(memory_space=pl.ANY), vmem],
             out_specs=(vmem, vmem),
@@ -688,6 +693,16 @@
                 collective_id=0, has_side_effects=True, vmem_limit_bytes=56 * 1024 * 1024
             ),
         )(coupling, initial)
+        return pl.pallas_call(
+            results_kernel,
+            name="results",
+            out_shape=(
+                jax.ShapeDtypeStruct((2, K, 64), F32),
+                jax.ShapeDtypeStruct((ITERS, 2, K, K), F32),
+            ),
+            in_specs=[vmem, vmem],
+            out_specs=(vmem, vmem),
+        )(value, projections)
 
     return jax.shard_map(
         body,

time: 113 us -> 111 us (0.982)
  local copies, waits for them, and re-layouts: 3.04 us -> 0 us
    unnamed x2 -> x0, local copies, waits for them, and re-layouts: 3.04 us -> none
    pallas_call x0 -> x1, Pallas kernels: none -> 1.69 us  [body(): pl.pallas_call(results_kernel, name='results', out_shape=(jax.ShapeDtypeS...]
where the time goes in v7:
time: 111 us
  Pallas kernels  110 us (99%)
    pallas_call x1, Pallas kernels, body(): pl.pallas_call(kernel, name='subspace', out_shape=(jax.ShapeDtypeStruct((...  108 us

profile of v7, /device:TPU:1, one launch (start us, length us, event | category | flops | bytes accessed | tf_op | source)
XLA Modules:
  0.0 110.7 jit_solution(17155091654052153578)
XLA Ops:
  0.6 108.4 %subspace.1 = (f32[48,128]{1,0:T(8,128)}, f32[192,128]{1,0:T(8,128)}) custom-call(f32[2,512,2048]{2,1,0:T(8,128)} %coupling.1, f32[2,48,512]{2,1,0:T(8,128)} %initial.1), custom_call_target="tpu_custom_call" | custom-call | tf_op jit(solution)/shard_map/subspace/pallas_call | solution.py:682
  109.0 1.7 %results.1 = (f32[2,48,64]{2,1,0:T(8,128)}, f32[4,2,48,48]{3,2,1,0:T(8,128)}) custom-call(f32[48,128]{1,0:T(8,128)} %get-tuple-element.4.value, f32[192,128]{1,0:T(8,128)} %get-tuple-element.5.projections), custom_call_target="tpu_custom_call" | custom-call | tf_op jit(solution)/shard_map/results/pallas_call | solution.py:696

commit v8 on v7

--- a/solution.py
+++ b/solution.py
@@ -455,6 +455,27 @@
             for k in range(1, C):
                 c_scatter(t, k).wait_send()
 
+    def slab(shift):
+        return pl.ds(pl.multiple_of(((c + shift) & 7) * RB, 8), RB)
+
+    def p_c(k):
+        return remote(psrc.at[slab(k)], py.at[k], py_s.at[k], py_r.at[k], at_c(k))
+
+    def p_x(j):
+        return remote(px.at[0], px.at[j], px_s.at[j], px_r.at[j], at_x(j))
+
+    def p_z(o):
+        return remote(pz.at[0], pz.at[o], pz_s.at[o], pz_r.at[o], at_z(o))
+
+    def p_all(k, shift):
+        return remote(pall.at[slab(shift)], pall.at[slab(shift)], pa_s.at[k], pa_r.at[k], at_c(k))
+
+    def added(total, n, copy, slots):
+        for i in range(1, n):
+            copy(i).wait_recv()
+            total = total + slots[i]
+        return total
+
     v_re, v_im = initial[0], initial[1]
     set_left(v_re, v_im)
     pl.semaphore_wait(barrier, len(partners))
@@ -507,13 +528,22 @@
     y1_piece = scattered(0)
     psrc[:K] = gram_packed(v_piece, y1_piece)
     psrc[K : 2 * K] = conj_apply_packed(inv1, gram_packed(y1_piece, y2_piece))
+    psrc[2 * K :] = jnp.zeros((2 * K, 128), F32)
+    for k in range(1, C):
+        p_c(k).start()
     column_sum()
     total = gzs[...]
     for o in range(1, Z):
         z_gram(o).wait_recv()
         total = total + gz[o]
     inv2 = column_gather(factor_start(unpack_triangle(total * (1.0 / N))))
+    px[0] = added(psrc[slab(0)], C, p_c, py)
+    for j in range(1, X):
+        p_x(j).start()
     row_product(1, embedded(inv2))
+    pz[0] = added(px[0], X, p_x, px)
+    for o in range(1, Z):
+        p_z(o).start()
     z4_piece = row_sum()
 
 
@@ -525,27 +555,6 @@
 
     def g_z(m, o):
         return remote(g4.at[m, 2], g4z.at[m, o], g4z_s.at[m, o], g4z_r.at[m, o], at_z(o))
-
-    def slab(shift):
-        return pl.ds(pl.multiple_of(((c + shift) & 7) * RB, 8), RB)
-
-    def p_c(k):
-        return remote(psrc.at[slab(k)], py.at[k], py_s.at[k], py_r.at[k], at_c(k))
-
-    def p_x(j):
-        return remote(px.at[0], px.at[j], px_s.at[j], px_r.at[j], at_x(j))
-
-    def p_z(o):
-        return remote(pz.at[0], pz.at[o], pz_s.at[o], pz_r.at[o], at_z(o))
-
-    def p_all(k, shift):
-        return remote(pall.at[slab(shift)], pall.at[slab(shift)], pa_s.at[k], pa_r.at[k], at_c(k))
-
-    def added(total, n, copy, slots):
-        for i in range(1, n):
-            copy(i).wait_recv()
-            total = total + slots[i]
-        return total
 
     def last_start(m, total):
         g4[m, 0] = total
@@ -580,50 +589,44 @@
     gram = last_start(0, pack_triangle(gram_packed(z4_piece, z4_piece)))
     y3_piece = scattered(1)
     projection = last_start(1, pack_triangle(gram_packed(y3_piece, z4_piece)))
-    psrc[2 * K : 3 * K] = conj_apply_packed(inv2, gram_packed(y2_piece, y3_piece))
-    psrc[3 * K :] = jnp.zeros((K, 128), F32)
-    for k in range(1, C):
-        p_c(k).start()
+    third = last_start(2, pack_triangle(conj_apply_packed(inv2, gram_packed(y2_piece, y3_piece))))
     inv3 = c_factor(1)
     gram = last_x(0, gram)
     y4_piece = apply_packed(inv3, z4_piece)
     projection = last_x(1, projection)
+    third = last_x(2, third)
     gram = last_z(0, gram)
-    px[0] = added(psrc[slab(0)], C, p_c, py)
-    for j in range(1, X):
-        p_x(j).start()
+    pall[slab(0)] = added(pz[0], Z, p_z, pz) * (1.0 / N)
+    for k in range(1, C):
+        p_all(k, 0).start()
     projection = last_z(1, projection)
-    pz[0] = added(px[0], X, p_x, px)
-    for o in range(1, Z):
-        p_z(o).start()
+    third = last_z(2, third)
     column_sent()
     row_sent(1)
     for k in range(1, C):
         c_whole(k, c).wait_send()
-        for m in range(2):
+        for m in range(3):
             g_c(m, k).wait_send()
         p_c(k).wait_send()
     for j in range(1, X):
         x_gram(j).wait_send()
-        for m in range(2):
+        for m in range(3):
             g_x(m, j).wait_send()
         p_x(j).wait_send()
     for o in range(1, Z):
         z_gram(o).wait_send()
     gram = both_sides(inv3, last_end(0, gram))
-    pall[slab(0)] = added(pz[0], Z, p_z, pz) * (1.0 / N)
-    for k in range(1, C):
-        p_all(k, 0).start()
     last_value[...] = apply_packed(inverse_factor(gram), y4_piece)
     last_projections[3 * K :] = both_sides(inv3, last_end(1, projection))
     for k in range(1, C):
         p_all(k, C - k).wait_recv()
-    last_projections[: 3 * K] = pall[: 3 * K]
+    last_projections[: 2 * K] = pall[: 2 * K]
+    last_projections[2 * K : 3 * K] = last_end(2, third)
 
     for k in range(1, C):
         p_all(k, 0).wait_send()
     for o in range(1, Z):
-        for m in range(2):
+        for m in range(3):
             g_z(m, o).wait_send()
         p_z(o).wait_send()
 
@@ -656,10 +659,10 @@
         pltpu.VMEM((X, *piece), F32),
         pltpu.VMEM(piece, F32),
         pltpu.VMEM((Z, *piece), F32),
-        pltpu.VMEM((2, 3, *piece), F32),
-        pltpu.VMEM((2, C, *piece), F32),
-        pltpu.VMEM((2, X, *piece), F32),
-        pltpu.VMEM((2, Z, *piece), F32),
+        pltpu.VMEM((3, 3, *piece), F32),
+        pltpu.VMEM((3, C, *piece), F32),
+        pltpu.VMEM((3, X, *piece), F32),
+        pltpu.VMEM((3, Z, *piece), F32),
         pltpu.VMEM((4 * K, 128), F32),
         pltpu.VMEM((C, *piece), F32),
         pltpu.VMEM((X, *piece), F32),
@@ -673,7 +676,7 @@
         dma((C,)), dma((C,)), dma((C,)), dma((C,)),
         dma((2, C)), dma((2,)), dma((2, C)), dma((2, C)),
         dma((X,)), dma((X,)), dma((Z,)), dma((Z,)),
-        dma((2, C)), dma((2, C)), dma((2, X)), dma((2, X)), dma((2, Z)), dma((2, Z)),
+        dma((3, C)), dma((3, C)), dma((3, X)), dma((3, X)), dma((3, Z)), dma((3, Z)),
         dma((C,)), dma((C,)), dma((X,)), dma((X,)), dma((Z,)), dma((Z,)), dma((C,)), dma((C,)),
     ]
     vmem = pl.BlockSpec(memory_space=pltpu.VMEM)

time: 111 us -> 109 us (0.982)
  Pallas kernels: 110 us -> 108 us
    pallas_call x1, Pallas kernels: 108 us -> 107 us  [body(): pl.pallas_call(kernel, name='subspace', out_shape=(jax.ShapeDtypeStruct((...]
where the time goes in v8:
time: 109 us
  Pallas kernels  108 us (99%)
    pallas_call x1, Pallas kernels, body(): pl.pallas_call(kernel, name='subspace', out_shape=(jax.ShapeDtypeStruct((...  107 us

profile of v8, /device:TPU:1, one launch (start us, length us, event | category | flops | bytes accessed | tf_op | source)
XLA Modules:
  0.0 109.0 jit_solution(10236803184916828037)
XLA Ops:
  0.6 106.7 %subspace.1 = (f32[48,128]{1,0:T(8,128)}, f32[192,128]{1,0:T(8,128)}) custom-call(f32[2,512,2048]{2,1,0:T(8,128)} %coupling.1, f32[2,48,512]{2,1,0:T(8,128)} %initial.1), custom_call_target="tpu_custom_call" | custom-call | tf_op jit(solution)/shard_map/subspace/pallas_call | solution.py:685
  107.3 1.7 %results.1 = (f32[2,48,64]{2,1,0:T(8,128)}, f32[4,2,48,48]{3,2,1,0:T(8,128)}) custom-call(f32[48,128]{1,0:T(8,128)} %get-tuple-element.4.value, f32[192,128]{1,0:T(8,128)} %get-tuple-element.5.projections), custom_call_target="tpu_custom_call" | custom-call | tf_op jit(solution)/shard_map/results/pallas_call | solution.py:699
